TPU v7x, 256 devices: a whole 4x4x8 slice. The times are simulated.
256 devices in a mesh: section: 8 (over y, x_lo), dp: 32 (over x_hi, z, core).
Axes of the slice: x: 4 (x_hi: 2, x_lo: 2; x = x_hi * 2 + x_lo), y: 4, z: 8, core: 2. Of those that a mesh axis runs over, the one named last changes fastest.
Arguments:
- embedded: bfloat16 [16384, 2048], P('dp'), may hold values from -6 to 6
- out_grad: bfloat16 [16384, 2048], P('dp'), may hold values from -0.046875 to 0.046875
- stored: bfloat16 [8, 2, 384, 64, 2048], P('section', None, 'dp'), as said below
- sample_ids: int32 [384], P('dp'), may hold values from 0 to 11, as said below
- lengths: int32 [384], P('dp'), may hold values from 1 to 64, as said below
- weight: bfloat16 [8, 2048, 2048], P('section', 'dp'), may hold values from -0.125 to 0.125
- gain: bfloat16 [8, 2048], P('section'), may hold values from 0.099609375 to 1.8984375
Outputs:
- boundary: bfloat16 [8, 16384, 2048], P('section', 'dp')
- weight_grad: float32 [8, 2048, 2048], P('section', 'dp')
Inputs may be any that keep to these rules, and one draw needn't show every extreme that they name: stored[s, 1] equals stored[s + 1, 0] for every s below the last block. `sample_ids`: within each data group's 12 entries every slot 0 to 11 appears once. In each data group the first 4 lengths (long bucket) lie in 33 to 64 and the rest in 1 to 32; each group has a long sample of length 64 and a short one of length 32.
All inputs are finite; a program needn't handle non-finite values.
Results may differ from a plain program's by a relative error of at most 0.027.
Values may be sent and summed in bfloat16 or wider, within the bound.
No kernel may reach another device: no remote copies, remote signals or barrier semaphores. Data moves between devices by JAX's collectives and lax.ppermute only.
A program may use at most 128 MiB of HBM per device.

v0:
```python
import jax
import jax.numpy as jnp
from jax import lax
from jax.sharding import PartitionSpec as P

QB = 128
LEN_A = 64
SPM_A = 1
MICRO = 4
LEN_B = 32
MB_TOK = 64


eps_norm = 1e-06
eps_scale = 1e-06


def from_behind(array, axis, by):
    length = lax.axis_size(axis)
    pairs = [(i, i + by) for i in range(length) if 0 <= i + by < length]
    return lax.ppermute(array, axis, pairs)


def quantize(values, block_size):
    row_count, feature_count = values.shape
    grouped = values.reshape(row_count, feature_count // block_size, block_size)
    scaling = (jnp.max(jnp.abs(grouped), axis=2) / 127.0 + eps_scale).astype(jnp.bfloat16)
    encoded = (grouped / scaling.astype(jnp.float32)[:, :, None]).astype(jnp.bfloat16)
    return (encoded.reshape(row_count, feature_count), scaling)


def restore(encoded, scaling, block_size):
    row_count, feature_count = encoded.shape
    grouped = encoded.astype(jnp.float32).reshape(
        row_count, feature_count // block_size, block_size
    )
    return (grouped * scaling.astype(jnp.float32)[:, :, None]).reshape(row_count, feature_count)


def normalize(block_in, gain_row):
    values = block_in.astype(jnp.float32)
    inverse = lax.rsqrt(jnp.mean(values * values, axis=1, keepdims=True) + eps_norm)
    return (values, inverse, values * inverse * gain_row)


def slot_rows(slot_data, slot_ids):
    count_long = MICRO * SPM_A
    feature_count = slot_data.shape[2]
    long_part = jnp.take(slot_data, slot_ids[:count_long], axis=0).reshape(-1, feature_count)
    short_part = jnp.take(slot_data, slot_ids[count_long:], axis=0)[:, :LEN_B].reshape(
        -1, feature_count
    )
    return jnp.concatenate([long_part, short_part], axis=0)


def live_rows(sample_len):
    count_long = MICRO * SPM_A
    count_short = sample_len.shape[0] - count_long
    place_long = jnp.tile(jnp.arange(LEN_A, dtype=jnp.int32), count_long)
    place_short = jnp.tile(jnp.arange(LEN_B, dtype=jnp.int32), count_short)
    limit_long = jnp.repeat(sample_len[:count_long], LEN_A)
    limit_short = jnp.repeat(sample_len[count_long:], LEN_B)
    return jnp.concatenate([place_long < limit_long, place_short < limit_short])


def body(embedded, out_grad, stored, sample_ids, lengths, weight, gain):
    sections = lax.axis_size("section")
    section_pos = lax.axis_index("section")
    features = embedded.shape[1]
    micro_total = 2 * MICRO
    batch_rows = MB_TOK
    full_weight = lax.all_gather(weight[0], "dp", axis=0, tiled=True)
    gain_row = gain[0].astype(jnp.float32)
    held_in = slot_rows(stored[0, 0], sample_ids).reshape(micro_total, batch_rows, features)
    held_out = slot_rows(stored[0, 1], sample_ids).reshape(micro_total, batch_rows, features)
    live = live_rows(lengths).reshape(micro_total, batch_rows, 1)
    first_in = embedded.reshape(micro_total, batch_rows, features)
    upstream = out_grad.reshape(micro_total, batch_rows, features)
    is_first = section_pos == 0
    is_last = section_pos == sections - 1
    blank_codes = jnp.zeros((batch_rows, features), jnp.bfloat16)
    blank_scales = jnp.zeros((batch_rows, features // QB), jnp.bfloat16)

    def forward_work(micro_index, encoded, scaling, stashed):
        inputs, normed_all, mixed_all, kept_all = stashed
        rebuilt = (held_in[micro_index].astype(jnp.float32) + restore(encoded, scaling, QB)).astype(
            jnp.bfloat16
        )
        block_in = jnp.where(is_first, first_in[micro_index], rebuilt)
        values, inverse, normal = normalize(block_in, gain_row)
        normed = normal.astype(jnp.bfloat16)
        mixed = jnp.dot(normed, full_weight, preferred_element_type=jnp.float32)
        output = values + jax.nn.silu(mixed)
        previous = held_out[micro_index].astype(jnp.float32)
        delta = jnp.where(live[micro_index], output - previous, 0.0)
        sent_codes, sent_scales = quantize(delta, QB)
        kept = jnp.where(is_last, output, previous + restore(sent_codes, sent_scales, QB)).astype(
            jnp.bfloat16
        )
        stashed = (
            inputs.at[micro_index].set(block_in),
            normed_all.at[micro_index].set(normed),
            mixed_all.at[micro_index].set(mixed),
            kept_all.at[micro_index].set(kept),
        )
        return (sent_codes, sent_scales, stashed)

    def forward_tick(micro_index, encoded, scaling, stashed):
        active = (micro_index >= 0) & (micro_index < micro_total)
        safe_index = jnp.clip(micro_index, 0, micro_total - 1)

        def forward_run_work(operands):
            return forward_work(safe_index, operands[0], operands[1], operands[2])

        def forward_skip_work(operands):
            return (blank_codes, blank_scales, operands[2])

        return lax.cond(active, forward_run_work, forward_skip_work, (encoded, scaling, stashed))

    def backward_work(micro_index, encoded, scaling, stashed, slopes):
        inputs, normed_all, mixed_all, kept_all = stashed
        given = jnp.where(live[micro_index], upstream[micro_index].astype(jnp.float32), 0.0)
        incoming = jnp.where(is_last, given, restore(encoded, scaling, QB))
        values, inverse, normal = normalize(inputs[micro_index], gain_row)
        mixed = mixed_all[micro_index]
        gated = jax.nn.sigmoid(mixed)
        slope = (incoming * gated * (1.0 + mixed * (1.0 - gated))).astype(jnp.bfloat16)
        back = lax.dot_general(
            slope, full_weight, (((1,), (1,)), ((), ())), preferred_element_type=jnp.float32
        )
        weighted = back * gain_row
        centre = jnp.mean(values * weighted, axis=1, keepdims=True)
        grad_in = incoming + inverse * weighted - values * inverse * inverse * inverse * centre
        sent_codes, sent_scales = quantize(grad_in, QB)
        return (sent_codes, sent_scales, slopes.at[micro_index].set(slope))

    def backward_tick(micro_index, encoded, scaling, stashed, slopes):
        active = (micro_index >= 0) & (micro_index < micro_total)
        safe_index = jnp.clip(micro_index, 0, micro_total - 1)

        def backward_run_work(operands):
            return backward_work(safe_index, operands[0], operands[1], operands[2], operands[3])

        def backward_skip_work(operands):
            return (blank_codes, blank_scales, operands[3])

        return lax.cond(
            active, backward_run_work, backward_skip_work, (encoded, scaling, stashed, slopes)
        )

    stashed = (
        jnp.zeros((micro_total, batch_rows, features), jnp.bfloat16),
        jnp.zeros((micro_total, batch_rows, features), jnp.bfloat16),
        jnp.zeros((micro_total, batch_rows, features), jnp.float32),
        jnp.zeros((micro_total, batch_rows, features), jnp.bfloat16),
    )
    slopes = jnp.zeros((micro_total, batch_rows, features), jnp.bfloat16)

    def ahead_step(moment, state):
        encoded, scaling, stashed_now = state
        encoded, scaling, stashed_now = forward_tick(
            moment - section_pos, encoded, scaling, stashed_now
        )
        encoded, scaling = from_behind((encoded, scaling), "section", 1)
        return (encoded, scaling, stashed_now)

    state = lax.fori_loop(
        0, micro_total + sections - 1, ahead_step, (blank_codes, blank_scales, stashed)
    )
    stashed = state[2]

    def behind_step(moment, state):
        back_codes, back_scales, slopes_now = state
        back_codes, back_scales, slopes_now = backward_tick(
            moment - (sections - 1 - section_pos), back_codes, back_scales, stashed, slopes_now
        )
        back_codes, back_scales = from_behind((back_codes, back_scales), "section", -1)
        return (back_codes, back_scales, slopes_now)

    state = lax.fori_loop(
        0, micro_total + sections - 1, behind_step, (blank_codes, blank_scales, slopes)
    )
    slopes = state[2]
    normed_rows = stashed[1].reshape(-1, features)
    slope_rows = slopes.reshape(-1, features)
    shard_grad = lax.psum_scatter(
        lax.dot_general(
            normed_rows, slope_rows, (((0,), (0,)), ((), ())), preferred_element_type=jnp.float32
        ).astype(jnp.bfloat16),
        "dp",
        scatter_dimension=0,
        tiled=True,
    ).astype(jnp.float32)
    return (stashed[3].reshape(1, -1, features), shard_grad[None])


def solution(mesh):
    in_specs = (
        P("dp", None),
        P("dp", None),
        P("section", None, "dp", None, None),
        P("dp"),
        P("dp"),
        P("section", "dp", None),
        P("section", None),
    )
    out_specs = (P("section", "dp", None), P("section", "dp", None))
    return jax.shard_map(body, mesh=mesh, in_specs=in_specs, out_specs=out_specs, check_vma=False)
```

profile of v0, /device:TPU:1, one launch (start us, length us, event | category | flops | bytes accessed | tf_op | source)
XLA Modules:
  0.0 1037.4 jit_solution(15517272339195394439)
XLA Ops:
  31.6 84.9 %all-gather.3.cloned.1.call-done = bf16[1,2048,2048]{2,1,0:T(8,128)(2,1)} async-done(((bf16[1,64,2048]{2,1,0:T(8,128)(2,1)}), bf16[1,2048,2048]{2,1,0:T(8,128)(2,1)}) %all-gather.3.cloned.1.call-update) | async-done | bytes 8388624 | tf_op jit(solution)/shard_map/all_gather | solution.py:72
  122.4 340.1 %while.50 = (s32[]{:T(128)}, bf16[64,2048]{1,0:T(8,128)(2,1)S(1)}, bf16[64,16]{1,0:T(8,128)(2,1)S(1)}, bf16[8,64,2048]{2,1,0:T(8,128)(2,1)S(1)}, bf16[8,64,2048]...) while((s32[]{:T(128)}, bf16[64,2048]{1,0:T(8,128)(2,1)S(1)}, ...), condition=%wide.region_6.9_spmd, body=%wide.region_0.8_spmd.sunk | while | flops 543033408 | bytes 20752940 | solution.py:167
  122.6 16.5 %conditional.4 = (bf16[64,2048]{1,0:T(8,128)(2,1)}, bf16[64,16]{1,0:T(8,128)(2,1)}, bf16[8,64,2048]{2,1,0:T(8,128)(2,1)S(1)}, bf16[8,64,2048]{2,1,0:T(8,128)(2,1...) conditional(s32[]{:T(128)} %convert_element_type.213, (bf16[8,64,2048]{2,1,0:T(8,128)(2,1)S(1)}, ...), branch_computations={%region_1.3_spmd, %region_2.7_spmd} | conditional | flops 543033408 | bytes 19695728 | solution.py:118
  126.4 6.5 fusion.9
  146.7 16.5 %conditional.4 = (bf16[64,2048]{1,0:T(8,128)(2,1)}, bf16[64,16]{1,0:T(8,128)(2,1)}, bf16[8,64,2048]{2,1,0:T(8,128)(2,1)S(1)}, bf16[8,64,2048]{2,1,0:T(8,128)(2,1...) conditional(s32[]{:T(128)} %convert_element_type.213, (bf16[8,64,2048]{2,1,0:T(8,128)(2,1)S(1)}, ...), branch_computations={%region_1.3_spmd, %region_2.7_spmd} | conditional | flops 543033408 | bytes 19695728 | solution.py:118
  150.4 6.5 fusion.9
  172.7 16.4 %conditional.4 = (bf16[64,2048]{1,0:T(8,128)(2,1)}, bf16[64,16]{1,0:T(8,128)(2,1)}, bf16[8,64,2048]{2,1,0:T(8,128)(2,1)S(1)}, bf16[8,64,2048]{2,1,0:T(8,128)(2,1...) conditional(s32[]{:T(128)} %convert_element_type.213, (bf16[8,64,2048]{2,1,0:T(8,128)(2,1)S(1)}, ...), branch_computations={%region_1.3_spmd, %region_2.7_spmd} | conditional | flops 543033408 | bytes 19695728 | solution.py:118
  176.4 6.5 fusion.9
  197.8 16.4 %conditional.4 = (bf16[64,2048]{1,0:T(8,128)(2,1)}, bf16[64,16]{1,0:T(8,128)(2,1)}, bf16[8,64,2048]{2,1,0:T(8,128)(2,1)S(1)}, bf16[8,64,2048]{2,1,0:T(8,128)(2,1...) conditional(s32[]{:T(128)} %convert_element_type.213, (bf16[8,64,2048]{2,1,0:T(8,128)(2,1)S(1)}, ...), branch_computations={%region_1.3_spmd, %region_2.7_spmd} | conditional | flops 543033408 | bytes 19695728 | solution.py:118
  201.5 6.5 fusion.9
  223.8 16.5 %conditional.4 = (bf16[64,2048]{1,0:T(8,128)(2,1)}, bf16[64,16]{1,0:T(8,128)(2,1)}, bf16[8,64,2048]{2,1,0:T(8,128)(2,1)S(1)}, bf16[8,64,2048]{2,1,0:T(8,128)(2,1...) conditional(s32[]{:T(128)} %convert_element_type.213, (bf16[8,64,2048]{2,1,0:T(8,128)(2,1)S(1)}, ...), branch_computations={%region_1.3_spmd, %region_2.7_spmd} | conditional | flops 543033408 | bytes 19695728 | solution.py:118
  227.6 6.5 fusion.9
  249.1 16.4 %conditional.4 = (bf16[64,2048]{1,0:T(8,128)(2,1)}, bf16[64,16]{1,0:T(8,128)(2,1)}, bf16[8,64,2048]{2,1,0:T(8,128)(2,1)S(1)}, bf16[8,64,2048]{2,1,0:T(8,128)(2,1...) conditional(s32[]{:T(128)} %convert_element_type.213, (bf16[8,64,2048]{2,1,0:T(8,128)(2,1)S(1)}, ...), branch_computations={%region_1.3_spmd, %region_2.7_spmd} | conditional | flops 543033408 | bytes 19695728 | solution.py:118
  252.9 6.5 fusion.9
  274.0 16.4 %conditional.4 = (bf16[64,2048]{1,0:T(8,128)(2,1)}, bf16[64,16]{1,0:T(8,128)(2,1)}, bf16[8,64,2048]{2,1,0:T(8,128)(2,1)S(1)}, bf16[8,64,2048]{2,1,0:T(8,128)(2,1...) conditional(s32[]{:T(128)} %convert_element_type.213, (bf16[8,64,2048]{2,1,0:T(8,128)(2,1)S(1)}, ...), branch_computations={%region_1.3_spmd, %region_2.7_spmd} | conditional | flops 543033408 | bytes 19695728 | solution.py:118
  277.7 6.5 fusion.9
  298.8 16.4 %conditional.4 = (bf16[64,2048]{1,0:T(8,128)(2,1)}, bf16[64,16]{1,0:T(8,128)(2,1)}, bf16[8,64,2048]{2,1,0:T(8,128)(2,1)S(1)}, bf16[8,64,2048]{2,1,0:T(8,128)(2,1...) conditional(s32[]{:T(128)} %convert_element_type.213, (bf16[8,64,2048]{2,1,0:T(8,128)(2,1)S(1)}, ...), branch_computations={%region_1.3_spmd, %region_2.7_spmd} | conditional | flops 543033408 | bytes 19695728 | solution.py:118
  302.6 6.5 fusion.9
  324.9 18.8 %collective-permute-start = (bf16[64,2048]{1,0:T(8,128)(2,1)}, bf16[64,2048]{1,0:T(8,128)(2,1)S(1)}, u32[]{:S(2)}, u32[]{:S(2)}) collective-permute-start(bf16[64,2048]{1,0:T(8,128)(2,1)} %get-tuple-element.1061), channel_id=1, source_target_pairs={{0,32},{32,64},{64,96},{96,128},{128,160},{160,192},{192,224},{1,3... | collective-permute-start | bytes 786440 | tf_op jit(solution)/shard_map/while/body/eval_jaxpr/ppermute | solution.py:21
  353.4 18.8 %collective-permute-start.1 = (bf16[64,16]{1,0:T(8,128)(2,1)}, bf16[64,16]{1,0:T(8,128)(2,1)S(1)}, u32[]{:S(2)}, u32[]{:S(2)}) collective-permute-start(bf16[64,16]{1,0:T(8,128)(2,1)} %get-tuple-element.1062), channel_id=1, source_target_pairs={{0,32},{32,64},{64,96},{96,128},{128,160},{160,192},{192,224},{1,3... | collective-permute-start | bytes 6152 | tf_op jit(solution)/shard_map/while/body/eval_jaxpr/ppermute | solution.py:21
  384.3 16.1 %collective-permute-start = (bf16[64,2048]{1,0:T(8,128)(2,1)}, bf16[64,2048]{1,0:T(8,128)(2,1)S(1)}, u32[]{:S(2)}, u32[]{:S(2)}) collective-permute-start(bf16[64,2048]{1,0:T(8,128)(2,1)} %get-tuple-element.1061), channel_id=1, source_target_pairs={{0,32},{32,64},{64,96},{96,128},{128,160},{160,192},{192,224},{1,3... | collective-permute-start | bytes 786440 | tf_op jit(solution)/shard_map/while/body/eval_jaxpr/ppermute | solution.py:21
  411.0 17.1 %collective-permute-start.1 = (bf16[64,16]{1,0:T(8,128)(2,1)}, bf16[64,16]{1,0:T(8,128)(2,1)S(1)}, u32[]{:S(2)}, u32[]{:S(2)}) collective-permute-start(bf16[64,16]{1,0:T(8,128)(2,1)} %get-tuple-element.1062), channel_id=1, source_target_pairs={{0,32},{32,64},{64,96},{96,128},{128,160},{160,192},{192,224},{1,3... | collective-permute-start | bytes 6152 | tf_op jit(solution)/shard_map/while/body/eval_jaxpr/ppermute | solution.py:21
  441.0 15.4 %collective-permute-start = (bf16[64,2048]{1,0:T(8,128)(2,1)}, bf16[64,2048]{1,0:T(8,128)(2,1)S(1)}, u32[]{:S(2)}, u32[]{:S(2)}) collective-permute-start(bf16[64,2048]{1,0:T(8,128)(2,1)} %get-tuple-element.1061), channel_id=1, source_target_pairs={{0,32},{32,64},{64,96},{96,128},{128,160},{160,192},{192,224},{1,3... | collective-permute-start | bytes 786440 | tf_op jit(solution)/shard_map/while/body/eval_jaxpr/ppermute | solution.py:21
  464.1 382.2 %while.51 = (s32[]{:T(128)}, bf16[64,2048]{1,0:T(8,128)(2,1)S(1)}, bf16[64,16]{1,0:T(8,128)(2,1)S(1)}, bf16[8,64,2048]{2,1,0:T(8,128)(2,1)}, s32[]{:T(128)}, /*i...) while((s32[]{:T(128)}, bf16[64,2048]{1,0:T(8,128)(2,1)S(1)}, ...), condition=%wide.region_14.17_spmd, body=%wide.region_7.16_spmd.sunk | while | flops 541853760 | bytes 19695792 | solution.py:180
  477.2 17.7 %collective-permute-done.3 = bf16[64,16]{1,0:T(8,128)(2,1)S(1)} collective-permute-done((bf16[64,16]{1,0:T(8,128)(2,1)}, bf16[64,16]{1,0:T(8,128)(2,1)S(1)}, u32[]{:S(2)}, u32[]{:S(2)}) %collective-permute-start.3) | collective-permute-done | bytes 2080 | tf_op jit(solution)/shard_map/while/body/eval_jaxpr/ppermute | solution.py:21
  518.2 16.8 %collective-permute-done.3 = bf16[64,16]{1,0:T(8,128)(2,1)S(1)} collective-permute-done((bf16[64,16]{1,0:T(8,128)(2,1)}, bf16[64,16]{1,0:T(8,128)(2,1)S(1)}, u32[]{:S(2)}, u32[]{:S(2)}) %collective-permute-start.3) | collective-permute-done | bytes 2080 | tf_op jit(solution)/shard_map/while/body/eval_jaxpr/ppermute | solution.py:21
  539.0 6.7 collective-permute-done.3
  549.6 97.4 %collective-permute-done.3 = bf16[64,16]{1,0:T(8,128)(2,1)S(1)} collective-permute-done((bf16[64,16]{1,0:T(8,128)(2,1)}, bf16[64,16]{1,0:T(8,128)(2,1)S(1)}, u32[]{:S(2)}, u32[]{:S(2)}) %collective-permute-start.3) | collective-permute-done | bytes 2080 | tf_op jit(solution)/shard_map/while/body/eval_jaxpr/ppermute | solution.py:21
  646.9 15.0 %conditional.5 = (bf16[64,2048]{1,0:T(8,128)(2,1)}, bf16[64,16]{1,0:T(8,128)(2,1)}, bf16[8,64,2048]{2,1,0:T(8,128)(2,1)}) conditional(s32[]{:T(128)} %convert_element_type.214, bf16[8,64,2048]{2,1,0:T(8,128)(2,1)} %get-tuple-element.1175, (pred[]{:T(512)}, s32[]{:T(128)}, pred[8,64,1]{1,2,0:T(4,128)(4,1)S(1)}, bf16[8,64,2048]{2,1,0:T(8,128)(2,1)}, ...), branch_computations={%region_8.10_spmd, %region_9.15_spmd} | conditional | flops 541853760 | bytes 18638678 | solution.py:147
  670.3 15.0 %conditional.5 = (bf16[64,2048]{1,0:T(8,128)(2,1)}, bf16[64,16]{1,0:T(8,128)(2,1)}, bf16[8,64,2048]{2,1,0:T(8,128)(2,1)}) conditional(s32[]{:T(128)} %convert_element_type.214, bf16[8,64,2048]{2,1,0:T(8,128)(2,1)} %get-tuple-element.1175, (pred[]{:T(512)}, s32[]{:T(128)}, pred[8,64,1]{1,2,0:T(4,128)(4,1)S(1)}, bf16[8,64,2048]{2,1,0:T(8,128)(2,1)}, ...), branch_computations={%region_8.10_spmd, %region_9.15_spmd} | conditional | flops 541853760 | bytes 18638678 | solution.py:147
  675.0 6.1 fusion.19
  687.9 6.7 collective-permute-done.3
  694.6 15.0 %conditional.5 = (bf16[64,2048]{1,0:T(8,128)(2,1)}, bf16[64,16]{1,0:T(8,128)(2,1)}, bf16[8,64,2048]{2,1,0:T(8,128)(2,1)}) conditional(s32[]{:T(128)} %convert_element_type.214, bf16[8,64,2048]{2,1,0:T(8,128)(2,1)} %get-tuple-element.1175, (pred[]{:T(512)}, s32[]{:T(128)}, pred[8,64,1]{1,2,0:T(4,128)(4,1)S(1)}, bf16[8,64,2048]{2,1,0:T(8,128)(2,1)}, ...), branch_computations={%region_8.10_spmd, %region_9.15_spmd} | conditional | flops 541853760 | bytes 18638678 | solution.py:147
  712.1 8.2 collective-permute-done.3
  720.3 15.0 %conditional.5 = (bf16[64,2048]{1,0:T(8,128)(2,1)}, bf16[64,16]{1,0:T(8,128)(2,1)}, bf16[8,64,2048]{2,1,0:T(8,128)(2,1)}) conditional(s32[]{:T(128)} %convert_element_type.214, bf16[8,64,2048]{2,1,0:T(8,128)(2,1)} %get-tuple-element.1175, (pred[]{:T(512)}, s32[]{:T(128)}, pred[8,64,1]{1,2,0:T(4,128)(4,1)S(1)}, bf16[8,64,2048]{2,1,0:T(8,128)(2,1)}, ...), branch_computations={%region_8.10_spmd, %region_9.15_spmd} | conditional | flops 541853760 | bytes 18638678 | solution.py:147
  725.0 6.1 fusion.19
  737.9 9.8 collective-permute-done.3
  747.7 15.0 %conditional.5 = (bf16[64,2048]{1,0:T(8,128)(2,1)}, bf16[64,16]{1,0:T(8,128)(2,1)}, bf16[8,64,2048]{2,1,0:T(8,128)(2,1)}) conditional(s32[]{:T(128)} %convert_element_type.214, bf16[8,64,2048]{2,1,0:T(8,128)(2,1)} %get-tuple-element.1175, (pred[]{:T(512)}, s32[]{:T(128)}, pred[8,64,1]{1,2,0:T(4,128)(4,1)S(1)}, bf16[8,64,2048]{2,1,0:T(8,128)(2,1)}, ...), branch_computations={%region_8.10_spmd, %region_9.15_spmd} | conditional | flops 541853760 | bytes 18638678 | solution.py:147
  765.2 8.7 collective-permute-done.3
  774.0 15.0 %conditional.5 = (bf16[64,2048]{1,0:T(8,128)(2,1)}, bf16[64,16]{1,0:T(8,128)(2,1)}, bf16[8,64,2048]{2,1,0:T(8,128)(2,1)}) conditional(s32[]{:T(128)} %convert_element_type.214, bf16[8,64,2048]{2,1,0:T(8,128)(2,1)} %get-tuple-element.1175, (pred[]{:T(512)}, s32[]{:T(128)}, pred[8,64,1]{1,2,0:T(4,128)(4,1)S(1)}, bf16[8,64,2048]{2,1,0:T(8,128)(2,1)}, ...), branch_computations={%region_8.10_spmd, %region_9.15_spmd} | conditional | flops 541853760 | bytes 18638678 | solution.py:147
  791.5 7.9 collective-permute-done.3
  799.4 15.0 %conditional.5 = (bf16[64,2048]{1,0:T(8,128)(2,1)}, bf16[64,16]{1,0:T(8,128)(2,1)}, bf16[8,64,2048]{2,1,0:T(8,128)(2,1)}) conditional(s32[]{:T(128)} %convert_element_type.214, bf16[8,64,2048]{2,1,0:T(8,128)(2,1)} %get-tuple-element.1175, (pred[]{:T(512)}, s32[]{:T(128)}, pred[8,64,1]{1,2,0:T(4,128)(4,1)S(1)}, bf16[8,64,2048]{2,1,0:T(8,128)(2,1)}, ...), branch_computations={%region_8.10_spmd, %region_9.15_spmd} | conditional | flops 541853760 | bytes 18638678 | solution.py:147
  804.0 6.1 fusion.19
  817.0 6.9 collective-permute-done.3
  823.8 15.0 %conditional.5 = (bf16[64,2048]{1,0:T(8,128)(2,1)}, bf16[64,16]{1,0:T(8,128)(2,1)}, bf16[8,64,2048]{2,1,0:T(8,128)(2,1)}) conditional(s32[]{:T(128)} %convert_element_type.214, bf16[8,64,2048]{2,1,0:T(8,128)(2,1)} %get-tuple-element.1175, (pred[]{:T(512)}, s32[]{:T(128)}, pred[8,64,1]{1,2,0:T(4,128)(4,1)S(1)}, bf16[8,64,2048]{2,1,0:T(8,128)(2,1)}, ...), branch_computations={%region_8.10_spmd, %region_9.15_spmd} | conditional | flops 541853760 | bytes 18638678 | solution.py:147
  828.5 6.1 fusion.19
  846.3 10.0 bitcast_convert_fusion
  856.3 172.4 %reduce-scatter.2.cloned.1.call-done = bf16[64,2048]{1,0:T(8,128)(2,1)} async-done(((bf16[2048,2048]{1,0:T(8,128)(2,1)}), bf16[64,2048]{1,0:T(8,128)(2,1)}) %reduce-scatter.2.cloned.1.call-update) | async-done | bytes 262160 | tf_op jit(solution)/shard_map/reduce_scatter | solution.py:186
  (382 shorter events, 423.4 us)
Async XLA Ops:
  7.2 109.3 %all-gather.3.cloned.1.call-start = ((), (), s32[]{:S(2)}) async-start(), calls=%async_computation.2 | async-start | bytes 8650752 | tf_op jit(solution)/shard_map/all_gather | solution.py:72
  7.9 1020.9 %reduce-scatter.2.cloned.1.call-start = ((), (), s32[]{:S(2)}) async-start(), calls=%async_computation.1 | async-start | bytes 8650752 | tf_op jit(solution)/shard_map/reduce_scatter | solution.py:186
  139.1 7.6 collective-permute-start
  163.2 9.5 collective-permute-start
  189.1 8.6 collective-permute-start
  214.2 9.6 collective-permute-start
  240.3 8.9 collective-permute-start
  265.6 8.4 collective-permute-start
  290.4 8.4 collective-permute-start
  315.3 8.4 collective-permute-start
  324.9 23.5 %collective-permute-start = (bf16[64,2048]{1,0:T(8,128)(2,1)}, bf16[64,2048]{1,0:T(8,128)(2,1)S(1)}, u32[]{:S(2)}, u32[]{:S(2)}) collective-permute-start(bf16[64,2048]{1,0:T(8,128)(2,1)} %get-tuple-element.1061), channel_id=1, source_target_pairs={{0,32},{32,64},{64,96},{96,128},{128,160},{160,192},{192,224},{1,3... | collective-permute-start | bytes 786440 | tf_op jit(solution)/shard_map/while/body/eval_jaxpr/ppermute | solution.py:21
  349.8 23.5 %collective-permute-start = (bf16[64,2048]{1,0:T(8,128)(2,1)}, bf16[64,2048]{1,0:T(8,128)(2,1)S(1)}, u32[]{:S(2)}, u32[]{:S(2)}) collective-permute-start(bf16[64,2048]{1,0:T(8,128)(2,1)} %get-tuple-element.1061), channel_id=1, source_target_pairs={{0,32},{32,64},{64,96},{96,128},{128,160},{160,192},{192,224},{1,3... | collective-permute-start | bytes 786440 | tf_op jit(solution)/shard_map/while/body/eval_jaxpr/ppermute | solution.py:21
  353.4 19.9 %collective-permute-start.1 = (bf16[64,16]{1,0:T(8,128)(2,1)}, bf16[64,16]{1,0:T(8,128)(2,1)S(1)}, u32[]{:S(2)}, u32[]{:S(2)}) collective-permute-start(bf16[64,16]{1,0:T(8,128)(2,1)} %get-tuple-element.1062), channel_id=1, source_target_pairs={{0,32},{32,64},{64,96},{96,128},{128,160},{160,192},{192,224},{1,3... | collective-permute-start | bytes 6152 | tf_op jit(solution)/shard_map/while/body/eval_jaxpr/ppermute | solution.py:21
  374.6 8.4 collective-permute-start
  384.3 21.7 %collective-permute-start = (bf16[64,2048]{1,0:T(8,128)(2,1)}, bf16[64,2048]{1,0:T(8,128)(2,1)S(1)}, u32[]{:S(2)}, u32[]{:S(2)}) collective-permute-start(bf16[64,2048]{1,0:T(8,128)(2,1)} %get-tuple-element.1061), channel_id=1, source_target_pairs={{0,32},{32,64},{64,96},{96,128},{128,160},{160,192},{192,224},{1,3... | collective-permute-start | bytes 786440 | tf_op jit(solution)/shard_map/while/body/eval_jaxpr/ppermute | solution.py:21
  407.4 21.8 %collective-permute-start = (bf16[64,2048]{1,0:T(8,128)(2,1)}, bf16[64,2048]{1,0:T(8,128)(2,1)S(1)}, u32[]{:S(2)}, u32[]{:S(2)}) collective-permute-start(bf16[64,2048]{1,0:T(8,128)(2,1)} %get-tuple-element.1061), channel_id=1, source_target_pairs={{0,32},{32,64},{64,96},{96,128},{128,160},{160,192},{192,224},{1,3... | collective-permute-start | bytes 786440 | tf_op jit(solution)/shard_map/while/body/eval_jaxpr/ppermute | solution.py:21
  411.0 18.1 %collective-permute-start.1 = (bf16[64,16]{1,0:T(8,128)(2,1)}, bf16[64,16]{1,0:T(8,128)(2,1)S(1)}, u32[]{:S(2)}, u32[]{:S(2)}) collective-permute-start(bf16[64,16]{1,0:T(8,128)(2,1)} %get-tuple-element.1062), channel_id=1, source_target_pairs={{0,32},{32,64},{64,96},{96,128},{128,160},{160,192},{192,224},{1,3... | collective-permute-start | bytes 6152 | tf_op jit(solution)/shard_map/while/body/eval_jaxpr/ppermute | solution.py:21
  430.5 9.2 collective-permute-start
  441.0 21.5 %collective-permute-start = (bf16[64,2048]{1,0:T(8,128)(2,1)}, bf16[64,2048]{1,0:T(8,128)(2,1)S(1)}, u32[]{:S(2)}, u32[]{:S(2)}) collective-permute-start(bf16[64,2048]{1,0:T(8,128)(2,1)} %get-tuple-element.1061), channel_id=1, source_target_pairs={{0,32},{32,64},{64,96},{96,128},{128,160},{160,192},{192,224},{1,3... | collective-permute-start | bytes 786440 | tf_op jit(solution)/shard_map/while/body/eval_jaxpr/ppermute | solution.py:21
  465.5 7.8 collective-permute-start.2
  466.8 6.5 collective-permute-start.3
  474.6 20.3 %collective-permute-start.2 = (bf16[64,2048]{1,0:T(8,128)(2,1)}, bf16[64,2048]{1,0:T(8,128)(2,1)S(1)}, u32[]{:S(2)}, u32[]{:S(2)}) collective-permute-start(bf16[64,2048]{1,0:T(8,128)(2,1)} %get-tuple-element.1079), channel_id=1, source_target_pairs={{32,0},{64,32},{96,64},{128,96},{160,128},{192,160},{224,192},{33,... | collective-permute-start | bytes 786440 | tf_op jit(solution)/shard_map/while/body/eval_jaxpr/ppermute | solution.py:21
  475.9 19.0 %collective-permute-start.3 = (bf16[64,16]{1,0:T(8,128)(2,1)}, bf16[64,16]{1,0:T(8,128)(2,1)S(1)}, u32[]{:S(2)}, u32[]{:S(2)}) collective-permute-start(bf16[64,16]{1,0:T(8,128)(2,1)} %get-tuple-element.1080), channel_id=1, source_target_pairs={{32,0},{64,32},{96,64},{128,96},{160,128},{192,160},{224,192},{33,... | collective-permute-start | bytes 6152 | tf_op jit(solution)/shard_map/while/body/eval_jaxpr/ppermute | solution.py:21
  496.2 8.4 collective-permute-start.2
  497.5 7.1 collective-permute-start.3
  505.9 8.4 collective-permute-start.2
  507.2 7.1 collective-permute-start.3
  515.7 19.4 %collective-permute-start.2 = (bf16[64,2048]{1,0:T(8,128)(2,1)}, bf16[64,2048]{1,0:T(8,128)(2,1)S(1)}, u32[]{:S(2)}, u32[]{:S(2)}) collective-permute-start(bf16[64,2048]{1,0:T(8,128)(2,1)} %get-tuple-element.1079), channel_id=1, source_target_pairs={{32,0},{64,32},{96,64},{128,96},{160,128},{192,160},{224,192},{33,... | collective-permute-start | bytes 786440 | tf_op jit(solution)/shard_map/while/body/eval_jaxpr/ppermute | solution.py:21
  516.9 18.1 %collective-permute-start.3 = (bf16[64,16]{1,0:T(8,128)(2,1)}, bf16[64,16]{1,0:T(8,128)(2,1)S(1)}, u32[]{:S(2)}, u32[]{:S(2)}) collective-permute-start(bf16[64,16]{1,0:T(8,128)(2,1)} %get-tuple-element.1080), channel_id=1, source_target_pairs={{32,0},{64,32},{96,64},{128,96},{160,128},{192,160},{224,192},{33,... | collective-permute-start | bytes 6152 | tf_op jit(solution)/shard_map/while/body/eval_jaxpr/ppermute | solution.py:21
  536.4 9.3 collective-permute-start.2
  537.6 8.0 collective-permute-start.3
  547.0 99.9 %collective-permute-start.2 = (bf16[64,2048]{1,0:T(8,128)(2,1)}, bf16[64,2048]{1,0:T(8,128)(2,1)S(1)}, u32[]{:S(2)}, u32[]{:S(2)}) collective-permute-start(bf16[64,2048]{1,0:T(8,128)(2,1)} %get-tuple-element.1079), channel_id=1, source_target_pairs={{32,0},{64,32},{96,64},{128,96},{160,128},{192,160},{224,192},{33,... | collective-permute-start | bytes 786440 | tf_op jit(solution)/shard_map/while/body/eval_jaxpr/ppermute | solution.py:21
  548.3 98.7 %collective-permute-start.3 = (bf16[64,16]{1,0:T(8,128)(2,1)}, bf16[64,16]{1,0:T(8,128)(2,1)S(1)}, u32[]{:S(2)}, u32[]{:S(2)}) collective-permute-start(bf16[64,16]{1,0:T(8,128)(2,1)} %get-tuple-element.1080), channel_id=1, source_target_pairs={{32,0},{64,32},{96,64},{128,96},{160,128},{192,160},{224,192},{33,... | collective-permute-start | bytes 6152 | tf_op jit(solution)/shard_map/while/body/eval_jaxpr/ppermute | solution.py:21
  661.9 8.4 collective-permute-start.2
  663.2 7.2 collective-permute-start.3
  685.3 9.2 collective-permute-start.2
  686.6 8.0 collective-permute-start.3
  709.5 10.8 %collective-permute-start.2 = (bf16[64,2048]{1,0:T(8,128)(2,1)}, bf16[64,2048]{1,0:T(8,128)(2,1)S(1)}, u32[]{:S(2)}, u32[]{:S(2)}) collective-permute-start(bf16[64,2048]{1,0:T(8,128)(2,1)} %get-tuple-element.1079), channel_id=1, source_target_pairs={{32,0},{64,32},{96,64},{128,96},{160,128},{192,160},{224,192},{33,... | collective-permute-start | bytes 786440 | tf_op jit(solution)/shard_map/while/body/eval_jaxpr/ppermute | solution.py:21
  710.8 9.5 collective-permute-start.3
  735.3 12.4 %collective-permute-start.2 = (bf16[64,2048]{1,0:T(8,128)(2,1)}, bf16[64,2048]{1,0:T(8,128)(2,1)S(1)}, u32[]{:S(2)}, u32[]{:S(2)}) collective-permute-start(bf16[64,2048]{1,0:T(8,128)(2,1)} %get-tuple-element.1079), channel_id=1, source_target_pairs={{32,0},{64,32},{96,64},{128,96},{160,128},{192,160},{224,192},{33,... | collective-permute-start | bytes 786440 | tf_op jit(solution)/shard_map/while/body/eval_jaxpr/ppermute | solution.py:21
  736.6 11.1 %collective-permute-start.3 = (bf16[64,16]{1,0:T(8,128)(2,1)}, bf16[64,16]{1,0:T(8,128)(2,1)S(1)}, u32[]{:S(2)}, u32[]{:S(2)}) collective-permute-start(bf16[64,16]{1,0:T(8,128)(2,1)} %get-tuple-element.1080), channel_id=1, source_target_pairs={{32,0},{64,32},{96,64},{128,96},{160,128},{192,160},{224,192},{33,... | collective-permute-start | bytes 6152 | tf_op jit(solution)/shard_map/while/body/eval_jaxpr/ppermute | solution.py:21
  762.6 11.3 %collective-permute-start.2 = (bf16[64,2048]{1,0:T(8,128)(2,1)}, bf16[64,2048]{1,0:T(8,128)(2,1)S(1)}, u32[]{:S(2)}, u32[]{:S(2)}) collective-permute-start(bf16[64,2048]{1,0:T(8,128)(2,1)} %get-tuple-element.1079), channel_id=1, source_target_pairs={{32,0},{64,32},{96,64},{128,96},{160,128},{192,160},{224,192},{33,... | collective-permute-start | bytes 786440 | tf_op jit(solution)/shard_map/while/body/eval_jaxpr/ppermute | solution.py:21
  763.9 10.1 collective-permute-start.3
  788.9 10.5 %collective-permute-start.2 = (bf16[64,2048]{1,0:T(8,128)(2,1)}, bf16[64,2048]{1,0:T(8,128)(2,1)S(1)}, u32[]{:S(2)}, u32[]{:S(2)}) collective-permute-start(bf16[64,2048]{1,0:T(8,128)(2,1)} %get-tuple-element.1079), channel_id=1, source_target_pairs={{32,0},{64,32},{96,64},{128,96},{160,128},{192,160},{224,192},{33,... | collective-permute-start | bytes 786440 | tf_op jit(solution)/shard_map/while/body/eval_jaxpr/ppermute | solution.py:21
  790.2 9.2 collective-permute-start.3
  814.4 9.5 collective-permute-start.2
  815.7 8.2 collective-permute-start.3
  838.8 7.5 collective-permute-start.2
  (19 other events, 90.4 us)
Sparse Core Ops, SparseCore 0:
  10.8 105.6 all-gather.2
  856.4 172.2 reduce-scatter.1
where the time goes:
time: 1050 us; the launch traced here: 1040 us
  waiting for transfers between devices  495 us (47%)
  starting transfers between devices  215 us (20%)
  other arithmetic  138 us (13%)
  matrix products  111 us (11%)
  local copies, waits for them, and re-layouts  62.4 us (6%)
  between operations  14.2 us (1%)
    ppermute x60, waiting for transfers between devices, from_behind(): return lax.ppermute(array, axis, pairs)  237 us
    ppermute x60, starting transfers between devices, from_behind(): return lax.ppermute(array, axis, pairs)  215 us
    reduce_scatter x1, waiting for transfers between devices, body(): lax.psum_scatter(lax.dot_general(normed_rows, slope_rows, (((0,), (0,)),...  172 us
    all_gather x1, waiting for transfers between devices, body(): full_weight = lax.all_gather(weight[0], 'dp', axis=0, tiled=True)  84.9 us
    dot_general x8, matrix products, forward_work(): mixed = jnp.dot(normed, full_weight, preferred_element_type=jnp.float32)  52 us
    dot_general x8, matrix products, backward_work(): lax.dot_general(slope, full_weight, (((1,), (1,)), ((), ())), preferred_e...  49.2 us
    scatter x8, other arithmetic, forward_work(): kept_all.at[micro_index].set(kept)  25.6 us
    scatter x8, other arithmetic, backward_work(): return (sent_codes, sent_scales, slopes.at[micro_index].set(slope))  24.1 us
  transfers between devices with their start and end apart: 62, of which 32 were waited for; matrix products, arithmetic and copies ran while one was open for 2% of the time, Pallas kernels for 0%

commit v1 on v0

v1 whole, which is shorter than its diff:
```python
import functools

import jax
import jax.numpy as jnp
from jax import lax
from jax.experimental import pallas as pl
from jax.experimental.pallas import tpu as pltpu
from jax.sharding import PartitionSpec as P

D = 2048
QTR = 32
N_MICRO = 4
ROWS = 128
N_SEC = 8
N_Z = 8
LAST = 10
TICKS = LAST + N_MICRO
EPS = 1e-6
BF = jnp.bfloat16
F32 = jnp.float32
BOTH = ("section", "dp")


def device(y, a, xh, z, c):
    return (2 * y + a) * 32 + 16 * xh + 2 * z + c


def pairs_of(target):
    out = []
    for y in range(4):
        for a in range(2):
            for xh in range(2):
                for z in range(N_Z):
                    for c in range(2):
                        to = target(y, a, xh, z, c)
                        if to is not None:
                            out.append((device(y, a, xh, z, c), device(*to)))
    return out


TURN = pairs_of(lambda y, a, xh, z, c: (y, c, xh, z, a))
TURN_FLIP = pairs_of(lambda y, a, xh, z, c: (y, 1 - c, xh, z, a))
TURN_FLIP_BACK = pairs_of(lambda y, a, xh, z, c: (y, c, xh, z, 1 - a))
CORES = pairs_of(lambda y, a, xh, z, c: (y, a, xh, z, 1 - c))
FAR_X = pairs_of(lambda y, a, xh, z, c: (y, a, 1 - xh, z, c))
UP_CORE = pairs_of(lambda y, a, xh, z, c: (y, a, xh, z, 1) if c == 0 else None)
UP_CHIP = pairs_of(lambda y, a, xh, z, c: (y + 1, a, xh, z, 0) if c == 1 and y < 3 else None)
DOWN_CORE = pairs_of(lambda y, a, xh, z, c: (y, a, xh, z, 0) if c == 1 else None)
DOWN_CHIP = pairs_of(lambda y, a, xh, z, c: (y - 1, a, xh, z, 1) if c == 0 and y > 0 else None)
Z_GROUPS = [[16 * xh + 2 * z + c for z in range(N_Z)] for xh in range(2) for c in range(2)]
X_GROUPS = [[16 * xh + 2 * z + c for xh in range(2)] for z in range(N_Z) for c in range(2)]

SHUFFLE = [(z * 2 + xh, xh * N_Z + z) for z in range(N_Z) for xh in range(2)]


def send(array, pairs):
    return lax.ppermute(array, BOTH, pairs)


def live_mask(tab, micro):
    row = lax.broadcasted_iota(jnp.int32, (ROWS, 1), 0)
    quarter = row // QTR
    limit = jnp.zeros((ROWS, 1), jnp.int32)
    for q in range(4):
        limit = jnp.where(quarter == q, tab[2 + micro * 4 + q], limit)
    return row - quarter * QTR < limit


def forward_kernel(
    tick, tab, first_ref, core_ref, chip_ref, held_ref, w_ref, gain_ref, sx, sm, sk,
    msg_ref, x_ref, mixed_ref, kept_ref, normed_ref,
):
    micro = tick - tab[1]
    block = tab[0]
    active = (micro >= 0) & (micro < N_MICRO)

    @pl.when(active & (block == 0))
    def _():
        x_ref[0] = first_ref[0]

    @pl.when(active & (block % 2 == 1))
    def _():
        x_ref[0] = core_ref[...]

    @pl.when(active & (block % 2 == 0) & (block > 0))
    def _():
        x_ref[0] = chip_ref[...]

    @pl.when(active)
    def _():
        values = x_ref[0].astype(F32)
        inverse = lax.rsqrt(jnp.mean(values * values, axis=1, keepdims=True) + EPS)
        normed = (values * inverse * gain_ref[...].astype(F32)).astype(BF)
        for to, at in SHUFFLE:
            normed_ref[:, to * 128 : to * 128 + 128] = normed[:, at * 128 : at * 128 + 128]
        mixed = jnp.dot(normed_ref[...], w_ref[...], preferred_element_type=F32)
        mixed_ref[0] = mixed
        output = x_ref[0].astype(F32) + mixed / (1.0 + jnp.exp(-mixed))
        keep = live_mask(tab, micro) | (block == N_SEC - 1)
        kept = jnp.where(keep, output, held_ref[0].astype(F32)).astype(BF)
        msg_ref[...] = kept
        kept_ref[0] = kept


def micro_block(tick, tab):
    return jnp.clip(tick - tab[1], 0, N_MICRO - 1)


def slot_block(tick, tab):
    micro = tick - tab[1]
    return jnp.where((micro >= 0) & (micro < N_MICRO), micro, N_MICRO)


ANY = pl.BlockSpec(memory_space=pl.ANY)
WHOLE = pl.BlockSpec((ROWS, D), lambda i, tab: (0, 0))
COST = pl.CostEstimate(flops=2 * ROWS * D * D, bytes_accessed=D * D * 2, transcendentals=ROWS * D)
PARAMS = pltpu.CompilerParams(vmem_limit_bytes=36 * 2**20)


def forward_tick(tick, tab, first, core, chip, held, weight, gain, stash):
    read = pl.BlockSpec((1, ROWS, D), lambda i, tab: (micro_block(tick, tab), 0, 0))
    slot = pl.BlockSpec((1, ROWS, D), lambda i, tab: (slot_block(tick, tab), 0, 0))
    return pl.pallas_call(
        functools.partial(forward_kernel, tick),
        grid_spec=pltpu.PrefetchScalarGridSpec(
            num_scalar_prefetch=1,
            grid=(1,),
            in_specs=[
                read, WHOLE, WHOLE, read,
                pl.BlockSpec((D, D), lambda i, tab: (0, 0)),
                pl.BlockSpec((1, D), lambda i, tab: (0, 0)),
                ANY, ANY, ANY,
            ],
            out_specs=[WHOLE, slot, slot, slot],
            scratch_shapes=[pltpu.VMEM((ROWS, D), BF)],
        ),
        out_shape=[jax.ShapeDtypeStruct((ROWS, D), BF)]
        + [jax.ShapeDtypeStruct(s.shape, s.dtype) for s in stash],
        input_output_aliases={7: 1, 8: 2, 9: 3},
        compiler_params=PARAMS,
        cost_estimate=COST,
        name=f"forward_{tick}",
    )(tab, first, core, chip, held, weight, gain, *stash)


def backward_kernel(
    tick, tab, given_ref, core_ref, chip_ref, w_ref, gain_ref, x_ref, mixed_ref, sn, ss,
    msg_ref, x_out, mixed_out, normed_ref, slope_ref, up_ref,
):
    micro = tick - (LAST - tab[1])
    block = tab[0]
    active = (micro >= 0) & (micro < N_MICRO)

    @pl.when(active & (block == N_SEC - 1))
    def _():
        given = given_ref[0].astype(F32)
        up_ref[...] = jnp.where(live_mask(tab, micro), given, 0.0).astype(BF)

    @pl.when(active & (block % 2 == 0))
    def _():
        up_ref[...] = core_ref[...]

    @pl.when(active & (block % 2 == 1) & (block < N_SEC - 1))
    def _():
        up_ref[...] = chip_ref[...]

    @pl.when(active)
    def _():
        mixed = mixed_ref[0]
        gated = 1.0 / (1.0 + jnp.exp(-mixed))
        up = up_ref[...].astype(F32)
        slope_ref[0] = (up * gated * (1.0 + mixed * (1.0 - gated))).astype(BF)
        values = x_ref[0].astype(F32)
        inverse = lax.rsqrt(jnp.mean(values * values, axis=1, keepdims=True) + EPS)
        normed = (values * inverse * gain_ref[...].astype(F32)).astype(BF)
        for to, at in SHUFFLE:
            normed_ref[0, :, to * 128 : to * 128 + 128] = normed[:, at * 128 : at * 128 + 128]

    @pl.when(active & (block > 0))
    def _():
        back = lax.dot_general(
            slope_ref[0], w_ref[...], (((1,), (1,)), ((), ())), preferred_element_type=F32
        )
        values = x_ref[0].astype(F32)
        inverse = lax.rsqrt(jnp.mean(values * values, axis=1, keepdims=True) + EPS)
        total = jnp.zeros((ROWS, 128), F32)
        weighted = []
        for to, at in SHUFFLE:
            part = back[:, to * 128 : to * 128 + 128] * gain_ref[:, at * 128 : at * 128 + 128].astype(F32)
            total = total + part * values[:, at * 128 : at * 128 + 128]
            weighted.append(part)
        centre = jnp.sum(total, axis=1, keepdims=True) * (1.0 / D)
        factor = inverse * inverse * inverse * centre
        for (to, at), part in zip(SHUFFLE, weighted):
            cols = slice(at * 128, at * 128 + 128)
            grad = up_ref[:, cols].astype(F32) + inverse * part - values[:, cols] * factor
            msg_ref[:, cols] = grad.astype(BF)


def backward_tick(tick, tab, given, core, chip, weight, gain, stash, sums):
    def micro_of(tab):
        return tick - (LAST - tab[1])

    def slot_of(tab):
        micro = micro_of(tab)
        return jnp.where((micro >= 0) & (micro < N_MICRO), micro, N_MICRO)

    read = pl.BlockSpec(
        (1, ROWS, D), lambda i, tab: (jnp.clip(micro_of(tab), 0, N_MICRO - 1), 0, 0)
    )
    slot = pl.BlockSpec((1, ROWS, D), lambda i, tab: (slot_of(tab), 0, 0))
    return pl.pallas_call(
        functools.partial(backward_kernel, tick),
        grid_spec=pltpu.PrefetchScalarGridSpec(
            num_scalar_prefetch=1,
            grid=(1,),
            in_specs=[
                read, WHOLE, WHOLE,
                pl.BlockSpec((D, D), lambda i, tab: (0, 0)),
                pl.BlockSpec((1, D), lambda i, tab: (0, 0)),
                read, read, ANY, ANY,
            ],
            out_specs=[WHOLE, ANY, ANY, slot, slot],
            scratch_shapes=[pltpu.VMEM((ROWS, D), BF)],
        ),
        out_shape=[jax.ShapeDtypeStruct((ROWS, D), BF)]
        + [jax.ShapeDtypeStruct(s.shape, s.dtype) for s in (*stash, *sums)],
        input_output_aliases={6: 1, 7: 2, 8: 3, 9: 4},
        compiler_params=PARAMS,
        cost_estimate=COST,
        name=f"backward_{tick}",
    )(tab, given, core, chip, weight, gain, *stash, *sums)


def held_rows(slots, ids):
    long_part = jnp.take(slots, ids[:4], axis=0).reshape(-1, D)
    short_part = jnp.take(slots[:, :QTR], ids[4:], axis=0).reshape(-1, D)
    return jnp.concatenate([long_part, short_part], axis=0)


def body(embedded, out_grad, stored, sample_ids, lengths, weight, gain):
    section = lax.axis_index("section")
    data = lax.axis_index("dp")
    y, a = section // 2, section % 2
    xh, c = data // 16, data % 2
    same = a == c
    block = 2 * y + c

    mine = send(weight[0], TURN)
    other = send(weight[0], TURN_FLIP)
    rows = jnp.where(
        a == 0, jnp.concatenate([mine, other], axis=0), jnp.concatenate([other, mine], axis=0)
    )
    rows = lax.all_gather(rows, "dp", axis=0, tiled=True, axis_index_groups=X_GROUPS)
    full = lax.all_gather(rows, "dp", axis=0, tiled=True, axis_index_groups=Z_GROUPS)

    ends = jnp.where(y == 0, embedded, out_grad)
    ends = jnp.where(same, ends, send(ends, CORES)).reshape(N_MICRO, ROWS, D)
    limits = jnp.where(same, lengths, send(lengths, CORES))
    gain_pair = jnp.where(same, gain, send(gain, TURN))
    held = send(held_rows(stored[0, 1], sample_ids), TURN).reshape(N_MICRO, ROWS, D)
    long_limits = jnp.stack([limits[:4], limits[:4] - QTR], axis=1).reshape(-1)
    tab = jnp.concatenate([jnp.stack([block, 3 * y + c]), long_limits, limits[4:]])

    blank = jnp.zeros((ROWS, D), BF)
    stash = [
        jnp.zeros((N_MICRO + 1, ROWS, D), BF),
        jnp.zeros((N_MICRO + 1, ROWS, D), F32),
        jnp.zeros((N_MICRO + 1, ROWS, D), BF),
    ]
    sums = [jnp.zeros((N_MICRO + 1, ROWS, D), BF), jnp.zeros((N_MICRO + 1, ROWS, D), BF)]
    up_core, up_chip = [blank], [blank, blank]
    down_core, down_chip = [blank], [blank, blank]
    kept = None
    for tick in range(LAST + TICKS):
        if tick < TICKS:
            msg, *stash = forward_tick(
                tick, tab, ends, up_core[tick], up_chip[tick], held, full, gain_pair, stash
            )
            if tick < TICKS - 1:
                up_core.append(send(msg, UP_CORE))
            if tick < TICKS - 2:
                up_chip.append(send(msg, UP_CHIP))
            if tick == TICKS - 1:
                kept = send(stash[2][:N_MICRO].reshape(-1, D), TURN)
                stash = stash[:2]
        if tick >= LAST:
            step = tick - LAST
            two = stash[:2]
            msg, two[0], two[1], *sums = backward_tick(
                step, tab, ends, down_core[step], down_chip[step], full, gain_pair, two, sums
            )
            stash = two + stash[2:]
            if step < TICKS - 1:
                down_core.append(send(msg, DOWN_CORE))
            if step < TICKS - 2:
                down_chip.append(send(msg, DOWN_CHIP))

    normed = sums[0][:N_MICRO].reshape(-1, D)
    slope = sums[1][:N_MICRO].reshape(-1, D)
    product = lax.dot_general(
        normed, slope, (((0,), (0,)), ((), ())), preferred_element_type=F32
    ).astype(BF)
    part = lax.psum_scatter(
        product, "dp", scatter_dimension=0, tiled=True, axis_index_groups=Z_GROUPS
    ).reshape(2, 128, D)
    own = lax.dynamic_index_in_dim(part, xh, 0, keepdims=False)
    far = send(lax.dynamic_index_in_dim(part, 1 - xh, 0, keepdims=False), FAR_X)
    both = (own.astype(F32) + far.astype(F32)).astype(BF).reshape(2, 64, D)
    first = send(lax.dynamic_index_in_dim(both, a, 0, keepdims=False), TURN)
    second = send(lax.dynamic_index_in_dim(both, 1 - a, 0, keepdims=False), TURN_FLIP_BACK)
    shard = first.astype(F32) + second.astype(F32)
    return (kept[None], shard[None])


def solution(mesh):
    in_specs = (
        P("dp", None),
        P("dp", None),
        P("section", None, "dp", None, None),
        P("dp"),
        P("dp"),
        P("section", "dp", None),
        P("section", None),
    )
    out_specs = (P("section", "dp", None), P("section", "dp", None))
    return jax.shard_map(body, mesh=mesh, in_specs=in_specs, out_specs=out_specs, check_vma=False)
```

time: 1050 us -> 553 us (0.53)
  waiting for transfers between devices: 495 us -> 228 us
  Pallas kernels: 0 us -> 139 us
  other arithmetic: 138 us -> 8.47 us
  matrix products: 111 us -> 6.83 us
  starting transfers between devices: 215 us -> 129 us
  local copies, waits for them, and re-layouts: 62.4 us -> 15.3 us
    ppermute x60, waiting for transfers between devices: 237 us -> 59.3 us  [send(): return lax.ppermute(array, BOTH, pairs)]
    pallas_call x0 -> x28, Pallas kernels: none -> 139 us  [the longest x14 73.9 us: backward_tick(): pl.pallas_call(functools.partial(backward_kernel, tick), grid_spec=pltpu....]
    dot_general x17 -> x1, matrix products: 111 us -> 6.83 us  [body(): lax.dot_general(normed, slope, (((0,), (0,)), ((), ())), preferred_elemen...]
    reduce_scatter x1, waiting for transfers between devices: 172 us -> 84.8 us  [body(): lax.psum_scatter(product, 'dp', scatter_dimension=0, tiled=True, axis_ind...]
    ppermute x60, starting transfers between devices: 215 us -> 129 us  [send(): return lax.ppermute(array, BOTH, pairs)]
    scatter x24 -> x0, other arithmetic: 65.6 us -> none  [the longest x8 25.6 us: forward_work(): kept_all.at[micro_index].set(kept)]
    another operation x16 -> x2, other arithmetic: 22.6 us -> 0.01 us  [body(): long_limits = jnp.stack([limits[:4], limits[:4] - QTR], axis=1).reshape(-1)]
    cond x16 -> x0, other arithmetic: 20.4 us -> none
  transfers between devices with their start and end apart: 62 -> 63, of which waited for: 32 -> 23; matrix products, arithmetic and copies ran while one was open for 2% -> 3% of each run, Pallas kernels for 0% -> 24%
where the time goes in v1:
time: 553 us; the launch traced here: 542 us
  waiting for transfers between devices  228 us (41%)
  Pallas kernels  139 us (25%)
  starting transfers between devices  129 us (23%)
  local copies, waits for them, and re-layouts  15.3 us (3%)
  between operations  15.2 us (3%)
  other arithmetic  8.47 us (2%)
  matrix products  6.83 us (1%)
    ppermute x60, starting transfers between devices, send(): return lax.ppermute(array, BOTH, pairs)  129 us
    reduce_scatter x1, waiting for transfers between devices, body(): lax.psum_scatter(product, 'dp', scatter_dimension=0, tiled=True, axis_ind...  84.8 us
    pallas_call x14, Pallas kernels, backward_tick(): pl.pallas_call(functools.partial(backward_kernel, tick), grid_spec=pltpu....  73.9 us
    pallas_call x14, Pallas kernels, forward_tick(): pl.pallas_call(functools.partial(forward_kernel, tick), grid_spec=pltpu.P...  65.2 us
    ppermute x60, waiting for transfers between devices, send(): return lax.ppermute(array, BOTH, pairs)  59.3 us
    all_gather x1, waiting for transfers between devices, body(): lax.all_gather(rows, 'dp', axis=0, tiled=True, axis_index_groups=Z_GROUPS)  53.6 us
    all_gather x1, waiting for transfers between devices, body(): lax.all_gather(rows, 'dp', axis=0, tiled=True, axis_index_groups=X_GROUPS)  29.8 us
  transfers between devices with their start and end apart: 63, of which 23 were waited for; matrix products, arithmetic and copies ran while one was open for 3% of the time, Pallas kernels for 24%

profile of v1, /device:TPU:1, one launch (start us, length us, event | category | flops | bytes accessed | tf_op | source)
XLA Modules:
  0.0 541.7 jit_solution(6615575058219937311)
XLA Ops:
  7.2 3.3 collective-permute-start.4
  13.3 5.1 collective-permute-done.3
  19.4 29.8 %all-gather.3.cloned.1.call-done = bf16[256,2048]{1,0:T(8,128)(2,1)} async-done(((bf16[128,2048]{1,0:T(8,128)(2,1)}), bf16[256,2048]{1,0:T(8,128)(2,1)}) %all-gather.3.cloned.1.call-update) | async-done | bytes 1048592 | tf_op jit(solution)/shard_map/all_gather | solution.py:254
  63.2 15.1 %collective-permute-start = (s32[12]{0:T(128)S(1)}, s32[12]{0:T(128)S(1)}, u32[]{:S(2)}, u32[]{:S(2)}) collective-permute-start(s32[12]{0:T(128)S(1)} %copy-done.5), channel_id=1, source_target_pairs={{0,1},{1,0},{2,3},{3,2},{4,5},{5,4},{6,7},{7,6},{8,9},{9,8},{10,11... | collective-permute-start | bytes 152 | tf_op jit(solution)/shard_map/ppermute | solution.py:57
  81.3 7.8 %collective-permute-done.5 = bf16[1,2048]{1,0:T(2,128)(2,1)S(1)} collective-permute-done((bf16[1,2048]{1,0:T(2,128)(2,1)S(1)}, bf16[1,2048]{1,0:T(2,128)(2,1)S(1)}, u32[]{:S(2)}, u32[]{:S(2)}) %collective-permute-start.5) | collective-permute-done | bytes 4128 | tf_op jit(solution)/shard_map/ppermute | solution.py:57
  91.1 53.6 %all-gather.5.cloned.1.call-done.w_ref = bf16[2048,2048]{1,0:T(8,128)(2,1)} async-done(((bf16[256,2048]{1,0:T(8,128)(2,1)}), bf16[2048,2048]{1,0:T(8,128)(2,1)}) %all-gather.5.cloned.1.call-update) | async-done | bytes 8388624 | tf_op jit(solution)/shard_map/all_gather | solution.py:255
  146.0 4.0 forward_0.1
  151.2 4.2 collective-permute-start.8
  155.4 5.8 %forward_1.1 = (bf16[128,2048]{1,0:T(8,128)(2,1)S(1)}, bf16[5,128,2048]{2,1,0:T(8,128)(2,1)S(1)}, f32[5,128,2048]{2,1,0:T(8,128)S(1)}, bf16[5,128,2048]{2,1,0:T(8,128)(2,1)S(1)}) custom-call(s32[18]{0:T(128)S(1)} %pad_add_fusion.1.tab, bf16[4,128,2048]{2,1,0:T(8,128)(2,1)S(1)} %bitcast.34, ...), custom_call_target="tpu_custom_call", output_to_operand_aliasing={{1}: (7, {}), {2}: (8, {}), {3}: (9, {})} | custom-call | flops 1073741824 | bytes 8388608 | tf_op jit(solution)/shard_map/forward_1/pallas_call | solution.py:123
  165.0 5.8 %forward_2.1 = (bf16[128,2048]{1,0:T(8,128)(2,1)S(1)}, bf16[5,128,2048]{2,1,0:T(8,128)(2,1)S(1)}, f32[5,128,2048]{2,1,0:T(8,128)S(1)}, bf16[5,128,2048]{2,1,0:T(8,128)(2,1)S(1)}) custom-call(s32[18]{0:T(128)S(1)} %pad_add_fusion.1.tab, bf16[4,128,2048]{2,1,0:T(8,128)(2,1)S(1)} %bitcast.35, ...), custom_call_target="tpu_custom_call", output_to_operand_aliasing={{1}: (7, {}), {2}: (8, {}), {3}: (9, {})} | custom-call | flops 1073741824 | bytes 8388608 | tf_op jit(solution)/shard_map/forward_2/pallas_call | solution.py:123
  174.7 6.3 %forward_3.1 = (bf16[128,2048]{1,0:T(8,128)(2,1)S(1)}, bf16[5,128,2048]{2,1,0:T(8,128)(2,1)S(1)}, f32[5,128,2048]{2,1,0:T(8,128)S(1)}, bf16[5,128,2048]{2,1,0:T(8,128)(2,1)S(1)}) custom-call(s32[18]{0:T(128)S(1)} %pad_add_fusion.1.tab, bf16[4,128,2048]{2,1,0:T(8,128)(2,1)S(1)} %bitcast.36, ...), custom_call_target="tpu_custom_call", output_to_operand_aliasing={{1}: (7, {}), {2}: (8, {}), {3}: (9, {})} | custom-call | flops 1073741824 | bytes 8388608 | tf_op jit(solution)/shard_map/forward_3/pallas_call | solution.py:123
  184.7 5.9 %forward_4.1 = (bf16[128,2048]{1,0:T(8,128)(2,1)S(1)}, bf16[5,128,2048]{2,1,0:T(8,128)(2,1)S(1)}, f32[5,128,2048]{2,1,0:T(8,128)S(1)}, bf16[5,128,2048]{2,1,0:T(8,128)(2,1)S(1)}) custom-call(s32[18]{0:T(128)S(1)} %pad_add_fusion.1.tab, bf16[4,128,2048]{2,1,0:T(8,128)(2,1)S(1)} %bitcast.37, ...), custom_call_target="tpu_custom_call", output_to_operand_aliasing={{1}: (7, {}), {2}: (8, {}), {3}: (9, {})} | custom-call | flops 1073741824 | bytes 8388608 | tf_op jit(solution)/shard_map/forward_4/pallas_call | solution.py:123
  194.4 4.1 forward_5.1
  202.4 4.1 forward_6.1
  207.7 4.2 collective-permute-start.20
  212.0 4.1 forward_7.1
  217.3 4.3 collective-permute-start.22
  221.6 4.1 forward_8.1
  229.5 4.2 forward_9.1
  237.7 4.1 forward_10.1
  243.7 3.9 backward_0.1
  247.6 3.1 collective-permute-start.29
  252.0 4.3 collective-permute-start.28
  256.4 4.1 forward_11.1
  261.7 4.1 backward_1.1
  265.9 3.1 collective-permute-start.32
  270.3 4.3 collective-permute-start.31
  274.6 4.1 forward_12.1
  280.0 3.9 backward_2.1
  288.3 4.9 forward_13.1
  293.2 4.7 backward_3.1
  300.7 3.9 backward_4.1
  309.7 3.9 backward_5.1
  317.4 4.1 backward_6.1
  325.5 3.9 backward_7.1
  333.4 3.9 backward_8.1
  339.9 14.3 %collective-permute-done.48.chip_ref = bf16[128,2048]{1,0:T(8,128)(2,1)S(1)} collective-permute-done((bf16[128,2048]{1,0:T(8,128)(2,1)S(1)}, bf16[128,2048]{1,0:T(8,128)(2,1)S(1)}, u32[]{:S(2)}, u32[]{:S(2)}) %collective-permute-start.48) | collective-permute-done | bytes 524320 | tf_op jit(solution)/shard_map/ppermute | solution.py:57
  354.2 8.3 %backward_9.1 = (bf16[128,2048]{1,0:T(8,128)(2,1)S(1)}, bf16[5,128,2048]{2,1,0:T(8,128)(2,1)S(1)}, f32[5,128,2048]{2,1,0:T(8,128)S(1)}, bf16[5,128,2048]{2,1,0:T(8,128)(2,1)S(1)}, bf16[5,128,2048]{2,1,0:T(8,128)(2,1)S(1)}) custom-call(s32[18]{0:T(128)S(1)} %pad_add_fusion.1.tab, ...), custom_call_target="tpu_custom_call", output_to_operand_aliasing={{1}: (6, {}), {2}: (7, {}), {3}: (8, {}), {4}: (9, {})} | custom-call | flops 1073741824 | bytes 8388608 | tf_op jit(solution)/shard_map/backward_9/pallas_call | solution.py:212
  366.1 8.1 %backward_10.1 = (bf16[128,2048]{1,0:T(8,128)(2,1)S(1)}, bf16[5,128,2048]{2,1,0:T(8,128)(2,1)S(1)}, f32[5,128,2048]{2,1,0:T(8,128)S(1)}, bf16[5,128,2048]{2,1,0:T(8,128)(2,1)S(1)}, bf16[5,128,2048]{2,1,0:T(8,128)(2,1)S(1)}) custom-call(s32[18]{0:T(128)S(1)} %pad_add_fusion.1.tab, ...), custom_call_target="tpu_custom_call", output_to_operand_aliasing={{1}: (6, {}), {2}: (7, {}), {3}: (8, {}), {4}: (9, {})} | custom-call | flops 1073741824 | bytes 8388608 | tf_op jit(solution)/shard_map/backward_10/pallas_call | solution.py:212
  378.2 8.1 %backward_11.1 = (bf16[128,2048]{1,0:T(8,128)(2,1)S(1)}, bf16[5,128,2048]{2,1,0:T(8,128)(2,1)S(1)}, f32[5,128,2048]{2,1,0:T(8,128)S(1)}, bf16[5,128,2048]{2,1,0:T(8,128)(2,1)S(1)}, bf16[5,128,2048]{2,1,0:T(8,128)(2,1)S(1)}) custom-call(s32[18]{0:T(128)S(1)} %pad_add_fusion.1.tab, ...), custom_call_target="tpu_custom_call", output_to_operand_aliasing={{1}: (6, {}), {2}: (7, {}), {3}: (8, {}), {4}: (9, {})} | custom-call | flops 1073741824 | bytes 8388608 | tf_op jit(solution)/shard_map/backward_11/pallas_call | solution.py:212
  390.1 8.3 %backward_12.1 = (bf16[128,2048]{1,0:T(8,128)(2,1)S(1)}, bf16[5,128,2048]{2,1,0:T(8,128)(2,1)S(1)}, f32[5,128,2048]{2,1,0:T(8,128)S(1)}, bf16[5,128,2048]{2,1,0:T(8,128)(2,1)S(1)}, bf16[5,128,2048]{2,1,0:T(8,128)(2,1)S(1)}) custom-call(s32[18]{0:T(128)S(1)} %pad_add_fusion.1.tab, ...), custom_call_target="tpu_custom_call", output_to_operand_aliasing={{1}: (6, {}), {2}: (7, {}), {3}: (8, {}), {4}: (9, {})} | custom-call | flops 1073741824 | bytes 8388608 | tf_op jit(solution)/shard_map/backward_12/pallas_call | solution.py:212
  401.3 4.7 backward_13.1
  406.0 6.8 %bitcast_convert_fusion = bf16[2048,2048]{1,0:T(8,128)(2,1)} fusion(bf16[5,128,2048]{2,1,0:T(8,128)(2,1)S(1)} %get-tuple-element.244, bf16[5,128,2048]{2,1,0:T(8,128)(2,1)S(1)} %get-tuple-element.245), kind=kOutput, calls=%fused_computation.2 | convolution fusion | flops 4299161600 | bytes 13107200 | tf_op jit(solution)/shard_map/dot_general | solution.py:301
  416.0 4.4 collective-permute-start.34
  420.5 84.8 %reduce-scatter.2.cloned.1.call-done = bf16[256,2048]{1,0:T(8,128)(2,1)} async-done(((bf16[2048,2048]{1,0:T(8,128)(2,1)}), bf16[256,2048]{1,0:T(8,128)(2,1)}) %reduce-scatter.2.cloned.1.call-update) | async-done | bytes 1048592 | tf_op jit(solution)/shard_map/reduce_scatter | solution.py:304
  509.1 11.6 %collective-permute-done.57 = bf16[128,2048]{1,0:T(8,128)(2,1)S(1)} collective-permute-done((bf16[128,2048]{1,0:T(8,128)(2,1)S(1)}, bf16[128,2048]{1,0:T(8,128)(2,1)S(1)}, u32[]{:S(2)}, u32[]{:S(2)}) %collective-permute-start.57) | collective-permute-done | bytes 524320 | tf_op jit(solution)/shard_map/ppermute | solution.py:57
  522.0 4.5 collective-permute-start.58
  526.6 3.9 collective-permute-done.58
  (161 shorter events, 114.7 us)
Async XLA Ops:
  7.2 42.0 %all-gather.3.cloned.1.call-start = ((), (), s32[]{:S(2)}) async-start(), calls=%async_computation.1 | async-start | bytes 1572864 | tf_op jit(solution)/shard_map/all_gather | solution.py:254
  7.2 6.1 %collective-permute-start.4 = (bf16[64,2048]{1,0:T(8,128)(2,1)}, bf16[64,2048]{1,0:T(8,128)(2,1)S(1)}, u32[]{:S(2)}, u32[]{:S(2)}) collective-permute-start(bf16[64,2048]{1,0:T(8,128)(2,1)} %bitcast.65), channel_id=1, source_target_pairs={{0,32},{1,0},{2,34},{3,2},{4,36},{5,4},{6,38},{7,6},{8,40},{9,8},{... | collective-permute-start | bytes 786440 | tf_op jit(solution)/shard_map/ppermute | solution.py:57
  10.5 7.9 %collective-permute-start.3 = (bf16[64,2048]{1,0:T(8,128)(2,1)}, bf16[64,2048]{1,0:T(8,128)(2,1)S(1)}, u32[]{:S(2)}, u32[]{:S(2)}) collective-permute-start(bf16[64,2048]{1,0:T(8,128)(2,1)} %bitcast.66), channel_id=1, source_target_pairs={{0,0},{1,32},{2,2},{3,34},{4,4},{5,36},{6,6},{7,38},{8,8},{9,40},{... | collective-permute-start | bytes 786440 | tf_op jit(solution)/shard_map/ppermute | solution.py:57
  19.4 125.3 %all-gather.5.cloned.1.call-start = ((), (), s32[]{:S(2)}) async-start(), calls=%async_computation.2 | async-start | bytes 9437184 | tf_op jit(solution)/shard_map/all_gather | solution.py:255
  49.2 456.1 %reduce-scatter.2.cloned.1.call-start = ((), (), s32[]{:S(2)}) async-start(), calls=%async_computation.3 | async-start | bytes 9437184 | tf_op jit(solution)/shard_map/reduce_scatter | solution.py:304
  50.9 38.3 %collective-permute-start.1 = (bf16[512,2048]{1,0:T(8,128)(2,1)}, bf16[512,2048]{1,0:T(8,128)(2,1)}, u32[]{:S(2)}, u32[]{:S(2)}) collective-permute-start(bf16[512,2048]{1,0:T(8,128)(2,1)} %broadcast_select_fusion), channel_id=1, source_target_pairs={{0,1},{1,0},{2,3},{3,2},{4,5},{5,4},{6,7},{7,6},{8,9},{9,8},{10,11... | collective-permute-start | bytes 6291464 | tf_op jit(solution)/shard_map/ppermute | solution.py:57
  61.1 29.9 %collective-permute-start.2 = (bf16[512,2048]{1,0:T(8,128)(2,1)}, bf16[512,2048]{1,0:T(8,128)(2,1)}, u32[]{:S(2)}, u32[]{:S(2)}) collective-permute-start(bf16[512,2048]{1,0:T(8,128)(2,1)} %pad_maximum_fusion), channel_id=1, source_target_pairs={{0,0},{1,32},{2,2},{3,34},{4,4},{5,36},{6,6},{7,38},{8,8},{9,40},{... | collective-permute-start | bytes 6291464 | tf_op jit(solution)/shard_map/ppermute | solution.py:57
  63.2 17.8 %collective-permute-start = (s32[12]{0:T(128)S(1)}, s32[12]{0:T(128)S(1)}, u32[]{:S(2)}, u32[]{:S(2)}) collective-permute-start(s32[12]{0:T(128)S(1)} %copy-done.5), channel_id=1, source_target_pairs={{0,1},{1,0},{2,3},{3,2},{4,5},{5,4},{6,7},{7,6},{8,9},{9,8},{10,11... | collective-permute-start | bytes 152 | tf_op jit(solution)/shard_map/ppermute | solution.py:57
  78.3 10.8 %collective-permute-start.5 = (bf16[1,2048]{1,0:T(2,128)(2,1)S(1)}, bf16[1,2048]{1,0:T(2,128)(2,1)S(1)}, u32[]{:S(2)}, u32[]{:S(2)}) collective-permute-start(bf16[1,2048]{1,0:T(2,128)(2,1)S(1)} %copy-done.4), channel_id=1, source_target_pairs={{0,0},{1,32},{2,2},{3,34},{4,4},{5,36},{6,6},{7,38},{8,8},{9,40},{... | collective-permute-start | bytes 12296 | tf_op jit(solution)/shard_map/ppermute | solution.py:57
  150.0 5.5 %collective-permute-start.6 = (bf16[128,2048]{1,0:T(8,128)(2,1)S(1)}, bf16[128,2048]{1,0:T(8,128)(2,1)S(1)}, u32[]{:S(2)}, u32[]{:S(2)}) collective-permute-start(bf16[128,2048]{1,0:T(8,128)(2,1)S(1)} %get-tuple-element.124), channel_id=1, source_target_pairs={{0,1},{2,3},{4,5},{6,7},{8,9},{10,11},{12,13},{14,15},{16,17},{18,... | collective-permute-start | bytes 1572872 | tf_op jit(solution)/shard_map/ppermute | solution.py:57
  151.2 13.7 %collective-permute-start.8 = (bf16[128,2048]{1,0:T(8,128)(2,1)S(1)}, bf16[128,2048]{1,0:T(8,128)(2,1)S(1)}, u32[]{:S(2)}, u32[]{:S(2)}) collective-permute-start(bf16[128,2048]{1,0:T(8,128)(2,1)S(1)} %get-tuple-element.124), channel_id=1, source_target_pairs={{1,64},{3,66},{5,68},{7,70},{9,72},{11,74},{13,76},{15,78},{17,80}... | collective-permute-start | bytes 1572872 | tf_op jit(solution)/shard_map/ppermute | solution.py:57
  162.5 11.5 %collective-permute-start.10 = (bf16[128,2048]{1,0:T(8,128)(2,1)S(1)}, bf16[128,2048]{1,0:T(8,128)(2,1)S(1)}, u32[]{:S(2)}, u32[]{:S(2)}) collective-permute-start(bf16[128,2048]{1,0:T(8,128)(2,1)S(1)} %get-tuple-element.128), channel_id=1, source_target_pairs={{1,64},{3,66},{5,68},{7,70},{9,72},{11,74},{13,76},{15,78},{17,80}... | collective-permute-start | bytes 1572872 | tf_op jit(solution)/shard_map/ppermute | solution.py:57
  172.1 11.4 %collective-permute-start.12 = (bf16[128,2048]{1,0:T(8,128)(2,1)S(1)}, bf16[128,2048]{1,0:T(8,128)(2,1)S(1)}, u32[]{:S(2)}, u32[]{:S(2)}) collective-permute-start(bf16[128,2048]{1,0:T(8,128)(2,1)S(1)} %get-tuple-element.132), channel_id=1, source_target_pairs={{1,64},{3,66},{5,68},{7,70},{9,72},{11,74},{13,76},{15,78},{17,80}... | collective-permute-start | bytes 1572872 | tf_op jit(solution)/shard_map/ppermute | solution.py:57
  182.2 11.0 %collective-permute-start.14 = (bf16[128,2048]{1,0:T(8,128)(2,1)S(1)}, bf16[128,2048]{1,0:T(8,128)(2,1)S(1)}, u32[]{:S(2)}, u32[]{:S(2)}) collective-permute-start(bf16[128,2048]{1,0:T(8,128)(2,1)S(1)} %get-tuple-element.136), channel_id=1, source_target_pairs={{1,64},{3,66},{5,68},{7,70},{9,72},{11,74},{13,76},{15,78},{17,80}... | collective-permute-start | bytes 1572872 | tf_op jit(solution)/shard_map/ppermute | solution.py:57
  191.9 10.5 %collective-permute-start.16 = (bf16[128,2048]{1,0:T(8,128)(2,1)S(1)}, bf16[128,2048]{1,0:T(8,128)(2,1)S(1)}, u32[]{:S(2)}, u32[]{:S(2)}) collective-permute-start(bf16[128,2048]{1,0:T(8,128)(2,1)S(1)} %get-tuple-element.140), channel_id=1, source_target_pairs={{1,64},{3,66},{5,68},{7,70},{9,72},{11,74},{13,76},{15,78},{17,80}... | collective-permute-start | bytes 1572872 | tf_op jit(solution)/shard_map/ppermute | solution.py:57
  199.8 12.2 %collective-permute-start.18 = (bf16[128,2048]{1,0:T(8,128)(2,1)S(1)}, bf16[128,2048]{1,0:T(8,128)(2,1)S(1)}, u32[]{:S(2)}, u32[]{:S(2)}) collective-permute-start(bf16[128,2048]{1,0:T(8,128)(2,1)S(1)} %get-tuple-element.144), channel_id=1, source_target_pairs={{1,64},{3,66},{5,68},{7,70},{9,72},{11,74},{13,76},{15,78},{17,80}... | collective-permute-start | bytes 1572872 | tf_op jit(solution)/shard_map/ppermute | solution.py:57
  206.4 5.5 %collective-permute-start.17 = (bf16[128,2048]{1,0:T(8,128)(2,1)S(1)}, bf16[128,2048]{1,0:T(8,128)(2,1)S(1)}, u32[]{:S(2)}, u32[]{:S(2)}) collective-permute-start(bf16[128,2048]{1,0:T(8,128)(2,1)S(1)} %get-tuple-element.148), channel_id=1, source_target_pairs={{0,1},{2,3},{4,5},{6,7},{8,9},{10,11},{12,13},{14,15},{16,17},{18,... | collective-permute-start | bytes 1572872 | tf_op jit(solution)/shard_map/ppermute | solution.py:57
  207.7 13.9 %collective-permute-start.20 = (bf16[128,2048]{1,0:T(8,128)(2,1)S(1)}, bf16[128,2048]{1,0:T(8,128)(2,1)S(1)}, u32[]{:S(2)}, u32[]{:S(2)}) collective-permute-start(bf16[128,2048]{1,0:T(8,128)(2,1)S(1)} %get-tuple-element.148), channel_id=1, source_target_pairs={{1,64},{3,66},{5,68},{7,70},{9,72},{11,74},{13,76},{15,78},{17,80}... | collective-permute-start | bytes 1572872 | tf_op jit(solution)/shard_map/ppermute | solution.py:57
  216.0 5.6 %collective-permute-start.19 = (bf16[128,2048]{1,0:T(8,128)(2,1)S(1)}, bf16[128,2048]{1,0:T(8,128)(2,1)S(1)}, u32[]{:S(2)}, u32[]{:S(2)}) collective-permute-start(bf16[128,2048]{1,0:T(8,128)(2,1)S(1)} %get-tuple-element.152), channel_id=1, source_target_pairs={{0,1},{2,3},{4,5},{6,7},{8,9},{10,11},{12,13},{14,15},{16,17},{18,... | collective-permute-start | bytes 1572872 | tf_op jit(solution)/shard_map/ppermute | solution.py:57
  217.3 12.2 %collective-permute-start.22 = (bf16[128,2048]{1,0:T(8,128)(2,1)S(1)}, bf16[128,2048]{1,0:T(8,128)(2,1)S(1)}, u32[]{:S(2)}, u32[]{:S(2)}) collective-permute-start(bf16[128,2048]{1,0:T(8,128)(2,1)S(1)} %get-tuple-element.152), channel_id=1, source_target_pairs={{1,64},{3,66},{5,68},{7,70},{9,72},{11,74},{13,76},{15,78},{17,80}... | collective-permute-start | bytes 1572872 | tf_op jit(solution)/shard_map/ppermute | solution.py:57
  227.0 10.7 %collective-permute-start.24 = (bf16[128,2048]{1,0:T(8,128)(2,1)S(1)}, bf16[128,2048]{1,0:T(8,128)(2,1)S(1)}, u32[]{:S(2)}, u32[]{:S(2)}) collective-permute-start(bf16[128,2048]{1,0:T(8,128)(2,1)S(1)} %get-tuple-element.156), channel_id=1, source_target_pairs={{1,64},{3,66},{5,68},{7,70},{9,72},{11,74},{13,76},{15,78},{17,80}... | collective-permute-start | bytes 1572872 | tf_op jit(solution)/shard_map/ppermute | solution.py:57
  235.0 21.3 %collective-permute-start.26 = (bf16[128,2048]{1,0:T(8,128)(2,1)S(1)}, bf16[128,2048]{1,0:T(8,128)(2,1)S(1)}, u32[]{:S(2)}, u32[]{:S(2)}) collective-permute-start(bf16[128,2048]{1,0:T(8,128)(2,1)S(1)} %get-tuple-element.160), channel_id=1, source_target_pairs={{1,64},{3,66},{5,68},{7,70},{9,72},{11,74},{13,76},{15,78},{17,80}... | collective-permute-start | bytes 1572872 | tf_op jit(solution)/shard_map/ppermute | solution.py:57
  241.8 14.6 %collective-permute-start.25 = (bf16[128,2048]{1,0:T(8,128)(2,1)S(1)}, bf16[128,2048]{1,0:T(8,128)(2,1)S(1)}, u32[]{:S(2)}, u32[]{:S(2)}) collective-permute-start(bf16[128,2048]{1,0:T(8,128)(2,1)S(1)} %get-tuple-element.164), channel_id=1, source_target_pairs={{0,1},{2,3},{4,5},{6,7},{8,9},{10,11},{12,13},{14,15},{16,17},{18,... | collective-permute-start | bytes 1572872 | tf_op jit(solution)/shard_map/ppermute | solution.py:57
  247.6 14.1 %collective-permute-start.29 = (bf16[128,2048]{1,0:T(8,128)(2,1)S(1)}, bf16[128,2048]{1,0:T(8,128)(2,1)S(1)}, u32[]{:S(2)}, u32[]{:S(2)}) collective-permute-start(bf16[128,2048]{1,0:T(8,128)(2,1)S(1)} %get-tuple-element.171), channel_id=1, source_target_pairs={{1,0},{3,2},{5,4},{7,6},{9,8},{11,10},{13,12},{15,14},{17,16},{19,... | collective-permute-start | bytes 1572872 | tf_op jit(solution)/shard_map/ppermute | solution.py:57
  250.7 29.3 %collective-permute-start.33 = (bf16[128,2048]{1,0:T(8,128)(2,1)S(1)}, bf16[128,2048]{1,0:T(8,128)(2,1)S(1)}, u32[]{:S(2)}, u32[]{:S(2)}) collective-permute-start(bf16[128,2048]{1,0:T(8,128)(2,1)S(1)} %get-tuple-element.171), channel_id=1, source_target_pairs={{64,1},{66,3},{68,5},{70,7},{72,9},{74,11},{76,13},{78,15},{80,17}... | collective-permute-start | bytes 1572872 | tf_op jit(solution)/shard_map/ppermute | solution.py:57
  252.0 18.2 %collective-permute-start.28 = (bf16[128,2048]{1,0:T(8,128)(2,1)S(1)}, bf16[128,2048]{1,0:T(8,128)(2,1)S(1)}, u32[]{:S(2)}, u32[]{:S(2)}) collective-permute-start(bf16[128,2048]{1,0:T(8,128)(2,1)S(1)} %get-tuple-element.164), channel_id=1, source_target_pairs={{1,64},{3,66},{5,68},{7,70},{9,72},{11,74},{13,76},{15,78},{17,80}... | collective-permute-start | bytes 1572872 | tf_op jit(solution)/shard_map/ppermute | solution.py:57
  260.4 14.2 %collective-permute-start.27 = (bf16[128,2048]{1,0:T(8,128)(2,1)S(1)}, bf16[128,2048]{1,0:T(8,128)(2,1)S(1)}, u32[]{:S(2)}, u32[]{:S(2)}) collective-permute-start(bf16[128,2048]{1,0:T(8,128)(2,1)S(1)} %get-tuple-element.170), channel_id=1, source_target_pairs={{0,1},{2,3},{4,5},{6,7},{8,9},{10,11},{12,13},{14,15},{16,17},{18,... | collective-permute-start | bytes 1572872 | tf_op jit(solution)/shard_map/ppermute | solution.py:57
  265.9 14.1 %collective-permute-start.32 = (bf16[128,2048]{1,0:T(8,128)(2,1)S(1)}, bf16[128,2048]{1,0:T(8,128)(2,1)S(1)}, u32[]{:S(2)}, u32[]{:S(2)}) collective-permute-start(bf16[128,2048]{1,0:T(8,128)(2,1)S(1)} %get-tuple-element.180), channel_id=1, source_target_pairs={{1,0},{3,2},{5,4},{7,6},{9,8},{11,10},{13,12},{15,14},{17,16},{19,... | collective-permute-start | bytes 1572872 | tf_op jit(solution)/shard_map/ppermute | solution.py:57
  269.0 24.2 %collective-permute-start.36 = (bf16[128,2048]{1,0:T(8,128)(2,1)S(1)}, bf16[128,2048]{1,0:T(8,128)(2,1)S(1)}, u32[]{:S(2)}, u32[]{:S(2)}) collective-permute-start(bf16[128,2048]{1,0:T(8,128)(2,1)S(1)} %get-tuple-element.180), channel_id=1, source_target_pairs={{64,1},{66,3},{68,5},{70,7},{72,9},{74,11},{76,13},{78,15},{80,17}... | collective-permute-start | bytes 1572872 | tf_op jit(solution)/shard_map/ppermute | solution.py:57
  270.3 18.0 %collective-permute-start.31 = (bf16[128,2048]{1,0:T(8,128)(2,1)S(1)}, bf16[128,2048]{1,0:T(8,128)(2,1)S(1)}, u32[]{:S(2)}, u32[]{:S(2)}) collective-permute-start(bf16[128,2048]{1,0:T(8,128)(2,1)S(1)} %get-tuple-element.170), channel_id=1, source_target_pairs={{1,64},{3,66},{5,68},{7,70},{9,72},{11,74},{13,76},{15,78},{17,80}... | collective-permute-start | bytes 1572872 | tf_op jit(solution)/shard_map/ppermute | solution.py:57
  278.7 9.6 %collective-permute-start.30 = (bf16[128,2048]{1,0:T(8,128)(2,1)S(1)}, bf16[128,2048]{1,0:T(8,128)(2,1)S(1)}, u32[]{:S(2)}, u32[]{:S(2)}) collective-permute-start(bf16[128,2048]{1,0:T(8,128)(2,1)S(1)} %get-tuple-element.179), channel_id=1, source_target_pairs={{0,1},{2,3},{4,5},{6,7},{8,9},{10,11},{12,13},{14,15},{16,17},{18,... | collective-permute-start | bytes 1572872 | tf_op jit(solution)/shard_map/ppermute | solution.py:57
  283.9 9.3 %collective-permute-start.35 = (bf16[128,2048]{1,0:T(8,128)(2,1)S(1)}, bf16[128,2048]{1,0:T(8,128)(2,1)S(1)}, u32[]{:S(2)}, u32[]{:S(2)}) collective-permute-start(bf16[128,2048]{1,0:T(8,128)(2,1)S(1)} %get-tuple-element.189), channel_id=1, source_target_pairs={{1,0},{3,2},{5,4},{7,6},{9,8},{11,10},{13,12},{15,14},{17,16},{19,... | collective-permute-start | bytes 1572872 | tf_op jit(solution)/shard_map/ppermute | solution.py:57
  287.0 13.5 %collective-permute-start.38 = (bf16[128,2048]{1,0:T(8,128)(2,1)S(1)}, bf16[128,2048]{1,0:T(8,128)(2,1)S(1)}, u32[]{:S(2)}, u32[]{:S(2)}) collective-permute-start(bf16[128,2048]{1,0:T(8,128)(2,1)S(1)} %get-tuple-element.189), channel_id=1, source_target_pairs={{64,1},{66,3},{68,5},{70,7},{72,9},{74,11},{76,13},{78,15},{80,17}... | collective-permute-start | bytes 1572872 | tf_op jit(solution)/shard_map/ppermute | solution.py:57
  299.2 10.5 %collective-permute-start.40 = (bf16[128,2048]{1,0:T(8,128)(2,1)S(1)}, bf16[128,2048]{1,0:T(8,128)(2,1)S(1)}, u32[]{:S(2)}, u32[]{:S(2)}) collective-permute-start(bf16[128,2048]{1,0:T(8,128)(2,1)S(1)} %get-tuple-element.194), channel_id=1, source_target_pairs={{64,1},{66,3},{68,5},{70,7},{72,9},{74,11},{76,13},{78,15},{80,17}... | collective-permute-start | bytes 1572872 | tf_op jit(solution)/shard_map/ppermute | solution.py:57
  304.6 5.1 collective-permute-start.39
  306.9 10.5 %collective-permute-start.42 = (bf16[128,2048]{1,0:T(8,128)(2,1)S(1)}, bf16[128,2048]{1,0:T(8,128)(2,1)S(1)}, u32[]{:S(2)}, u32[]{:S(2)}) collective-permute-start(bf16[128,2048]{1,0:T(8,128)(2,1)S(1)} %get-tuple-element.199), channel_id=1, source_target_pairs={{64,1},{66,3},{68,5},{70,7},{72,9},{74,11},{76,13},{78,15},{80,17}... | collective-permute-start | bytes 1572872 | tf_op jit(solution)/shard_map/ppermute | solution.py:57
  315.0 10.5 %collective-permute-start.44 = (bf16[128,2048]{1,0:T(8,128)(2,1)S(1)}, bf16[128,2048]{1,0:T(8,128)(2,1)S(1)}, u32[]{:S(2)}, u32[]{:S(2)}) collective-permute-start(bf16[128,2048]{1,0:T(8,128)(2,1)S(1)} %get-tuple-element.204), channel_id=1, source_target_pairs={{64,1},{66,3},{68,5},{70,7},{72,9},{74,11},{76,13},{78,15},{80,17}... | collective-permute-start | bytes 1572872 | tf_op jit(solution)/shard_map/ppermute | solution.py:57
  322.9 10.5 %collective-permute-start.46 = (bf16[128,2048]{1,0:T(8,128)(2,1)S(1)}, bf16[128,2048]{1,0:T(8,128)(2,1)S(1)}, u32[]{:S(2)}, u32[]{:S(2)}) collective-permute-start(bf16[128,2048]{1,0:T(8,128)(2,1)S(1)} %get-tuple-element.209), channel_id=1, source_target_pairs={{64,1},{66,3},{68,5},{70,7},{72,9},{74,11},{76,13},{78,15},{80,17}... | collective-permute-start | bytes 1572872 | tf_op jit(solution)/shard_map/ppermute | solution.py:57
  330.7 23.5 %collective-permute-start.48 = (bf16[128,2048]{1,0:T(8,128)(2,1)S(1)}, bf16[128,2048]{1,0:T(8,128)(2,1)S(1)}, u32[]{:S(2)}, u32[]{:S(2)}) collective-permute-start(bf16[128,2048]{1,0:T(8,128)(2,1)S(1)} %get-tuple-element.214), channel_id=1, source_target_pairs={{64,1},{66,3},{68,5},{70,7},{72,9},{74,11},{76,13},{78,15},{80,17}... | collective-permute-start | bytes 1572872 | tf_op jit(solution)/shard_map/ppermute | solution.py:57
  337.3 16.9 %collective-permute-start.47 = (bf16[128,2048]{1,0:T(8,128)(2,1)S(1)}, bf16[128,2048]{1,0:T(8,128)(2,1)S(1)}, u32[]{:S(2)}, u32[]{:S(2)}) collective-permute-start(bf16[128,2048]{1,0:T(8,128)(2,1)S(1)} %get-tuple-element.219), channel_id=1, source_target_pairs={{1,0},{3,2},{5,4},{7,6},{9,8},{11,10},{13,12},{15,14},{17,16},{19,... | collective-permute-start | bytes 1572872 | tf_op jit(solution)/shard_map/ppermute | solution.py:57
  338.6 27.5 %collective-permute-start.50 = (bf16[128,2048]{1,0:T(8,128)(2,1)S(1)}, bf16[128,2048]{1,0:T(8,128)(2,1)S(1)}, u32[]{:S(2)}, u32[]{:S(2)}) collective-permute-start(bf16[128,2048]{1,0:T(8,128)(2,1)S(1)} %get-tuple-element.219), channel_id=1, source_target_pairs={{64,1},{66,3},{68,5},{70,7},{72,9},{74,11},{76,13},{78,15},{80,17}... | collective-permute-start | bytes 1572872 | tf_op jit(solution)/shard_map/ppermute | solution.py:57
  363.8 14.4 %collective-permute-start.52 = (bf16[128,2048]{1,0:T(8,128)(2,1)S(1)}, bf16[128,2048]{1,0:T(8,128)(2,1)S(1)}, u32[]{:S(2)}, u32[]{:S(2)}) collective-permute-start(bf16[128,2048]{1,0:T(8,128)(2,1)S(1)} %get-tuple-element.224), channel_id=1, source_target_pairs={{64,1},{66,3},{68,5},{70,7},{72,9},{74,11},{76,13},{78,15},{80,17}... | collective-permute-start | bytes 1572872 | tf_op jit(solution)/shard_map/ppermute | solution.py:57
  375.5 14.6 %collective-permute-start.54 = (bf16[128,2048]{1,0:T(8,128)(2,1)S(1)}, bf16[128,2048]{1,0:T(8,128)(2,1)S(1)}, u32[]{:S(2)}, u32[]{:S(2)}) collective-permute-start(bf16[128,2048]{1,0:T(8,128)(2,1)S(1)} %get-tuple-element.229), channel_id=1, source_target_pairs={{64,1},{66,3},{68,5},{70,7},{72,9},{74,11},{76,13},{78,15},{80,17}... | collective-permute-start | bytes 1572872 | tf_op jit(solution)/shard_map/ppermute | solution.py:57
  387.6 12.2 %collective-permute-start.56 = (bf16[128,2048]{1,0:T(8,128)(2,1)S(1)}, bf16[128,2048]{1,0:T(8,128)(2,1)S(1)}, u32[]{:S(2)}, u32[]{:S(2)}) collective-permute-start(bf16[128,2048]{1,0:T(8,128)(2,1)S(1)} %get-tuple-element.234), channel_id=1, source_target_pairs={{64,1},{66,3},{68,5},{70,7},{72,9},{74,11},{76,13},{78,15},{80,17}... | collective-permute-start | bytes 1572872 | tf_op jit(solution)/shard_map/ppermute | solution.py:57
  416.0 110.6 %collective-permute-start.34 = (bf16[512,2048]{1,0:T(8,128)(2,1)}, bf16[512,2048]{1,0:T(8,128)(2,1)S(1)}, u32[]{:S(2)}, u32[]{:S(2)}) collective-permute-start(bf16[512,2048]{1,0:T(8,128)(2,1)} %bitcast.10), channel_id=1, source_target_pairs={{0,0},{1,32},{2,2},{3,34},{4,4},{5,36},{6,6},{7,38},{8,8},{9,40},{... | collective-permute-start | bytes 6291464 | tf_op jit(solution)/shard_map/ppermute | solution.py:57
  506.4 14.4 %collective-permute-start.57 = (bf16[128,2048]{1,0:T(8,128)(2,1)S(1)}, bf16[128,2048]{1,0:T(8,128)(2,1)S(1)}, u32[]{:S(2)}, u32[]{:S(2)}) collective-permute-start(bf16[128,2048]{1,0:T(8,128)(2,1)S(1)} %dynamic-slice_bitcast_fusion), channel_id=1, source_target_pairs={{0,16},{1,17},{2,18},{3,19},{4,20},{5,21},{6,22},{7,23},{8,24},{9,... | collective-permute-start | bytes 1572872 | tf_op jit(solution)/shard_map/ppermute | solution.py:57
  522.0 8.5 %collective-permute-start.58 = (bf16[64,2048]{1,0:T(8,128)(2,1)S(1)}, bf16[64,2048]{1,0:T(8,128)(2,1)S(1)}, u32[]{:S(2)}, u32[]{:S(2)}) collective-permute-start(bf16[64,2048]{1,0:T(8,128)(2,1)S(1)} %get-tuple-element.250), channel_id=1, source_target_pairs={{0,0},{1,32},{2,2},{3,34},{4,4},{5,36},{6,6},{7,38},{8,8},{9,40},{... | collective-permute-start | bytes 786440 | tf_op jit(solution)/shard_map/ppermute | solution.py:57
  526.5 6.1 %collective-permute-start.59 = (bf16[64,2048]{1,0:T(8,128)(2,1)S(1)}, bf16[64,2048]{1,0:T(8,128)(2,1)S(1)}, u32[]{:S(2)}, u32[]{:S(2)}) collective-permute-start(bf16[64,2048]{1,0:T(8,128)(2,1)S(1)} %get-tuple-element.251), channel_id=1, source_target_pairs={{0,1},{1,33},{2,3},{3,35},{4,5},{5,37},{6,7},{7,39},{8,9},{9,41},{... | collective-permute-start | bytes 786440 | tf_op jit(solution)/shard_map/ppermute | solution.py:57
  (22 other events, 131.1 us)
Sparse Core Ops, SparseCore 0:
  19.5 29.6 all-gather.2
  51.0 93.6 all-gather.4
  413.0 92.2 reduce-scatter.1

commit v2 on v1

v2 whole, which is shorter than its diff:
```python
import functools

import jax
import jax.numpy as jnp
from jax import lax
from jax.experimental import pallas as pl
from jax.experimental.pallas import tpu as pltpu
from jax.sharding import PartitionSpec as P

D = 2048
QTR = 32
N_MICRO = 4
ROWS = 128
N_SEC = 8
N_Z = 8
LAST = 10
TICKS = LAST + N_MICRO
EPS = 1e-6
BF = jnp.bfloat16
F32 = jnp.float32
BOTH = ("section", "dp")


def device(y, a, xh, z, c):
    return (2 * y + a) * 32 + 16 * xh + 2 * z + c


def pairs_of(target):
    out = []
    for y in range(4):
        for a in range(2):
            for xh in range(2):
                for z in range(N_Z):
                    for c in range(2):
                        to = target(y, a, xh, z, c)
                        if to is not None:
                            out.append((device(y, a, xh, z, c), device(*to)))
    return out


TURN = pairs_of(lambda y, a, xh, z, c: (y, c, xh, z, a))
CORES = pairs_of(lambda y, a, xh, z, c: (y, a, xh, z, 1 - c))
UP_CORE = pairs_of(lambda y, a, xh, z, c: (y, a, xh, z, 1) if c == 0 else None)
UP_CHIP = pairs_of(lambda y, a, xh, z, c: (y + 1, a, xh, z, 0) if c == 1 and y < 3 else None)
DOWN_CORE = pairs_of(lambda y, a, xh, z, c: (y, a, xh, z, 0) if c == 1 else None)
DOWN_CHIP = pairs_of(lambda y, a, xh, z, c: (y - 1, a, xh, z, 1) if c == 0 and y > 0 else None)
RIGHT = pairs_of(lambda y, a, xh, z, c: (y, a, xh, (z + 1) % N_Z, c))
LEFT = pairs_of(lambda y, a, xh, z, c: (y, a, xh, (z - 1) % N_Z, c))
FLIPS = [(dx, dt) for dx in range(2) for dt in range(2)]
TO_ROLE = [pairs_of(lambda y, a, xh, z, c: (y, c ^ dt, xh ^ dx, z, a)) for dx, dt in FLIPS]
TO_PLACE = [pairs_of(lambda y, a, xh, z, c: (y, c, xh ^ dx, z, a ^ dt)) for dx, dt in FLIPS]

CHUNK = 256
HALF = 1024


def send(array, pairs):
    return lax.ppermute(array, BOTH, pairs)


ANY = pl.BlockSpec(memory_space=pl.ANY)
WHOLE = pl.BlockSpec((ROWS, D), lambda i, tab: (0, 0))
COST = pl.CostEstimate(flops=2 * ROWS * D * D, bytes_accessed=D * D * 2, transcendentals=ROWS * D)
PARAMS = pltpu.CompilerParams(vmem_limit_bytes=30 * 2**20)


def feature_columns(z, k, xh):
    return pl.ds(pl.multiple_of((xh * N_Z + lax.rem(z + k, N_Z)) * 128, 128), 128)


def arrange_kernel(place, p0, p1, p2, p3, left_ref, right_ref):
    for (dx, dt), part in zip(FLIPS, (p0, p1, p2, p3)):
        index = (place[0] ^ dx) * 2 + (place[1] ^ dt)
        rows = pl.ds(pl.multiple_of(index * 64, 64), 64)
        left_ref[rows, :] = part[:, :HALF]
        right_ref[rows, :] = part[:, HALF:]


def arrange(place, parts):
    half = jax.ShapeDtypeStruct((CHUNK, HALF), BF)
    return pl.pallas_call(
        arrange_kernel,
        grid_spec=pltpu.PrefetchScalarGridSpec(
            num_scalar_prefetch=1,
            grid=(1,),
            in_specs=[pl.BlockSpec((64, D), lambda i, place: (0, 0))] * 4,
            out_specs=[pl.BlockSpec((CHUNK, HALF), lambda i, place: (0, 0))] * 2,
        ),
        out_shape=[half, half],
        name="arrange",
    )(place, *parts)


def assemble_kernel(*refs):
    out = refs[-1]
    for k in range(N_Z):
        for h in range(2):
            out[k * CHUNK : (k + 1) * CHUNK, h * HALF : (h + 1) * HALF] = refs[2 * k + h][...]


def assemble(chunks):
    return pl.pallas_call(
        assemble_kernel,
        grid=(1,),
        in_specs=[pl.BlockSpec((CHUNK, HALF), lambda i: (0, 0))] * 16,
        out_specs=pl.BlockSpec((D, D), lambda i: (0, 0)),
        out_shape=jax.ShapeDtypeStruct((D, D), BF),
        compiler_params=PARAMS,
        name="assemble",
    )(*[half for chunk in chunks for half in chunk])


def gather_weight(place, shard):
    own = arrange(place, [send(shard, pairs) for pairs in TO_ROLE])
    chunks = [None] * N_Z
    chunks[0] = list(own)
    from_left, from_right = list(own), list(own)
    for step in range(1, 4):
        from_left = [send(half, RIGHT) for half in from_left]
        from_right = [send(half, LEFT) for half in from_right]
        chunks[N_Z - step], chunks[step] = from_left, from_right
    chunks[4] = [send(from_left[0], RIGHT), send(from_right[1], LEFT)]
    return assemble(chunks)


def product_kernel(has, n_ref, s_ref, *refs):
    rows = N_MICRO * ROWS
    total = lax.dot_general(
        n_ref[...].reshape(rows, CHUNK),
        s_ref[...].reshape(rows, HALF),
        (((0,), (0,)), ((), ())),
        preferred_element_type=F32,
    )
    for ref in refs[:has]:
        total = total + ref[...].astype(F32)
    refs[has][...] = total.astype(BF)


def product(sums, k, half, arrived):
    piece = pl.BlockSpec((CHUNK, HALF), lambda i: (0, 0))
    return pl.pallas_call(
        functools.partial(product_kernel, len(arrived)),
        grid=(1,),
        in_specs=[
            pl.BlockSpec((N_MICRO, ROWS, CHUNK), lambda i: (0, 0, k)),
            pl.BlockSpec((N_MICRO, ROWS, HALF), lambda i: (0, 0, half)),
        ]
        + [piece] * len(arrived),
        out_specs=piece,
        out_shape=jax.ShapeDtypeStruct((CHUNK, HALF), BF),
        compiler_params=PARAMS,
        cost_estimate=pl.CostEstimate(
            flops=2 * N_MICRO * ROWS * CHUNK * HALF, bytes_accessed=2**21, transcendentals=0
        ),
        name=f"product_{k}_{half}",
    )(*sums, *arrived)


def spread_kernel(place, left_ref, right_ref, o0, o1, o2, o3):
    for (dx, dt), out in zip(FLIPS, (o0, o1, o2, o3)):
        index = (place[0] ^ dx) * 2 + (place[1] ^ dt)
        rows = pl.ds(pl.multiple_of(index * 64, 64), 64)
        out[:, :HALF] = left_ref[rows, :]
        out[:, HALF:] = right_ref[rows, :]


def spread(place, halves):
    return pl.pallas_call(
        spread_kernel,
        grid_spec=pltpu.PrefetchScalarGridSpec(
            num_scalar_prefetch=1,
            grid=(1,),
            in_specs=[pl.BlockSpec((CHUNK, HALF), lambda i, place: (0, 0))] * 2,
            out_specs=[pl.BlockSpec((64, D), lambda i, place: (0, 0))] * 4,
        ),
        out_shape=[jax.ShapeDtypeStruct((64, D), BF)] * 4,
        name="spread",
    )(place, *halves)


def scatter_grad(place, sums):
    to_right = [send(product(sums, 4, 0, []), RIGHT), None]
    to_left = [None, send(product(sums, 4, 1, []), LEFT)]
    for step in range(3, 0, -1):
        for half in (1, 0):
            held = to_right[half]
            to_right[half] = send(product(sums, step, half, [] if held is None else [held]), RIGHT)
            held = to_left[1 - half]
            to_left[1 - half] = send(
                product(sums, N_Z - step, 1 - half, [] if held is None else [held]), LEFT
            )
    halves = [product(sums, 0, half, [to_right[half], to_left[half]]) for half in range(2)]
    parts = [send(part, pairs) for part, pairs in zip(spread(place, halves), TO_PLACE)]
    total = parts[0].astype(F32)
    for part in parts[1:]:
        total = total + part.astype(F32)
    return total


def live_mask(tab, micro):
    row = lax.broadcasted_iota(jnp.int32, (ROWS, 1), 0)
    quarter = row // QTR
    limit = jnp.zeros((ROWS, 1), jnp.int32)
    for q in range(4):
        limit = jnp.where(quarter == q, tab[3 + micro * 4 + q], limit)
    return row - quarter * QTR < limit


def forward_kernel(
    tick, tab, first_ref, core_ref, chip_ref, held_ref, w_ref, gain_ref, sx, sm, sk, sn,
    msg_ref, x_ref, mixed_ref, kept_ref, normed_ref, plain_ref,
):
    micro = tick - tab[1]
    block = tab[0]
    active = (micro >= 0) & (micro < N_MICRO)

    @pl.when(active & (block == 0))
    def _():
        x_ref[0] = first_ref[0]

    @pl.when(active & (block % 2 == 1))
    def _():
        x_ref[0] = core_ref[...]

    @pl.when(active & (block % 2 == 0) & (block > 0))
    def _():
        x_ref[0] = chip_ref[...]

    @pl.when(active)
    def _():
        values = x_ref[0].astype(F32)
        inverse = lax.rsqrt(jnp.mean(values * values, axis=1, keepdims=True) + EPS)
        plain_ref[...] = (values * inverse * gain_ref[...].astype(F32)).astype(BF)
        for k in range(N_Z):
            for xh in range(2):
                to = k * CHUNK + xh * 128
                normed_ref[0, :, to : to + 128] = plain_ref[:, feature_columns(tab[2], k, xh)]
        mixed = jnp.dot(normed_ref[0], w_ref[...], preferred_element_type=F32)
        mixed_ref[0] = mixed
        output = x_ref[0].astype(F32) + mixed / (1.0 + jnp.exp(-mixed))
        keep = live_mask(tab, micro) | (block == N_SEC - 1)
        kept = jnp.where(keep, output, held_ref[0].astype(F32)).astype(BF)
        msg_ref[...] = kept
        kept_ref[0] = kept


def micro_block(tick, tab):
    return jnp.clip(tick - tab[1], 0, N_MICRO - 1)


def slot_block(tick, tab):
    micro = tick - tab[1]
    return jnp.where((micro >= 0) & (micro < N_MICRO), micro, N_MICRO)


def forward_tick(tick, tab, first, core, chip, held, weight, gain, stash):
    read = pl.BlockSpec((1, ROWS, D), lambda i, tab: (micro_block(tick, tab), 0, 0))
    slot = pl.BlockSpec((1, ROWS, D), lambda i, tab: (slot_block(tick, tab), 0, 0))
    return pl.pallas_call(
        functools.partial(forward_kernel, tick),
        grid_spec=pltpu.PrefetchScalarGridSpec(
            num_scalar_prefetch=1,
            grid=(1,),
            in_specs=[
                read, WHOLE, WHOLE, read,
                pl.BlockSpec((D, D), lambda i, tab: (0, 0)),
                pl.BlockSpec((1, D), lambda i, tab: (0, 0)),
                ANY, ANY, ANY, ANY,
            ],
            out_specs=[WHOLE, slot, slot, slot, slot],
            scratch_shapes=[pltpu.VMEM((ROWS, D), BF)],
        ),
        out_shape=[jax.ShapeDtypeStruct((ROWS, D), BF)]
        + [jax.ShapeDtypeStruct(s.shape, s.dtype) for s in stash],
        input_output_aliases={7: 1, 8: 2, 9: 3, 10: 4},
        compiler_params=PARAMS,
        cost_estimate=COST,
        name=f"forward_{tick}",
    )(tab, first, core, chip, held, weight, gain, *stash)


def backward_kernel(
    tick, tab, given_ref, core_ref, chip_ref, w_ref, gain_ref, x_ref, mixed_ref, ss,
    msg_ref, x_out, mixed_out, slope_ref, up_ref,
):
    micro = tick - (LAST - tab[1])
    block = tab[0]
    active = (micro >= 0) & (micro < N_MICRO)

    @pl.when(active & (block == N_SEC - 1))
    def _():
        given = given_ref[0].astype(F32)
        up_ref[...] = jnp.where(live_mask(tab, micro), given, 0.0).astype(BF)

    @pl.when(active & (block % 2 == 0))
    def _():
        up_ref[...] = core_ref[...]

    @pl.when(active & (block % 2 == 1) & (block < N_SEC - 1))
    def _():
        up_ref[...] = chip_ref[...]

    @pl.when(active)
    def _():
        mixed = mixed_ref[0]
        gated = 1.0 / (1.0 + jnp.exp(-mixed))
        up = up_ref[...].astype(F32)
        slope_ref[0] = (up * gated * (1.0 + mixed * (1.0 - gated))).astype(BF)

    @pl.when(active & (block > 0))
    def _():
        back = lax.dot_general(
            slope_ref[0], w_ref[...], (((1,), (1,)), ((), ())), preferred_element_type=F32
        )
        values = x_ref[0].astype(F32)
        inverse = lax.rsqrt(jnp.mean(values * values, axis=1, keepdims=True) + EPS)
        total = jnp.zeros((ROWS, 128), F32)
        weighted = []
        for k in range(N_Z):
            for xh in range(2):
                cols = feature_columns(tab[2], k, xh)
                at = k * CHUNK + xh * 128
                part = back[:, at : at + 128] * gain_ref[:, cols].astype(F32)
                total = total + part * x_ref[0, :, cols].astype(F32)
                weighted.append((cols, part))
        centre = jnp.sum(total, axis=1, keepdims=True) * (1.0 / D)
        factor = inverse * inverse * inverse * centre
        for cols, part in weighted:
            grad = up_ref[:, cols].astype(F32) + inverse * part
            msg_ref[:, cols] = (grad - x_ref[0, :, cols].astype(F32) * factor).astype(BF)


def backward_tick(tick, tab, given, core, chip, weight, gain, stash, slopes):
    def micro_of(tab):
        return tick - (LAST - tab[1])

    def slot_of(tab):
        micro = micro_of(tab)
        return jnp.where((micro >= 0) & (micro < N_MICRO), micro, N_MICRO)

    read = pl.BlockSpec(
        (1, ROWS, D), lambda i, tab: (jnp.clip(micro_of(tab), 0, N_MICRO - 1), 0, 0)
    )
    slot = pl.BlockSpec((1, ROWS, D), lambda i, tab: (slot_of(tab), 0, 0))
    return pl.pallas_call(
        functools.partial(backward_kernel, tick),
        grid_spec=pltpu.PrefetchScalarGridSpec(
            num_scalar_prefetch=1,
            grid=(1,),
            in_specs=[
                read, WHOLE, WHOLE,
                pl.BlockSpec((D, D), lambda i, tab: (0, 0)),
                pl.BlockSpec((1, D), lambda i, tab: (0, 0)),
                read, read, ANY,
            ],
            out_specs=[WHOLE, ANY, ANY, slot],
            scratch_shapes=[pltpu.VMEM((ROWS, D), BF)],
        ),
        out_shape=[jax.ShapeDtypeStruct((ROWS, D), BF)]
        + [jax.ShapeDtypeStruct(s.shape, s.dtype) for s in (*stash, slopes)],
        input_output_aliases={6: 1, 7: 2, 8: 3},
        compiler_params=PARAMS,
        cost_estimate=COST,
        name=f"backward_{tick}",
    )(tab, given, core, chip, weight, gain, *stash, slopes)


def held_rows(slots, ids):
    long_part = jnp.take(slots, ids[:4], axis=0).reshape(-1, D)
    short_part = jnp.take(slots[:, :QTR], ids[4:], axis=0).reshape(-1, D)
    return jnp.concatenate([long_part, short_part], axis=0)


def body(embedded, out_grad, stored, sample_ids, lengths, weight, gain):
    section = lax.axis_index("section")
    data = lax.axis_index("dp")
    y, a = section // 2, section % 2
    xh, c = data // 16, data % 2
    z = (data // 2) % N_Z
    same = a == c
    block = 2 * y + c
    place = jnp.stack([xh, a, z])
    full = gather_weight(place, weight[0])

    ends = jnp.where(y == 0, embedded, out_grad)
    ends = jnp.where(same, ends, send(ends, CORES)).reshape(N_MICRO, ROWS, D)
    limits = jnp.where(same, lengths, send(lengths, CORES))
    gain_pair = send(gain, TURN)
    held = send(held_rows(stored[0, 1], sample_ids), TURN).reshape(N_MICRO, ROWS, D)
    long_limits = jnp.stack([limits[:4], limits[:4] - QTR], axis=1).reshape(-1)
    tab = jnp.concatenate([jnp.stack([block, 3 * y + c, z]), long_limits, limits[4:]])

    blank = jnp.zeros((ROWS, D), BF)
    stash = [
        jnp.zeros((N_MICRO + 1, ROWS, D), BF),
        jnp.zeros((N_MICRO + 1, ROWS, D), F32),
        jnp.zeros((N_MICRO + 1, ROWS, D), BF),
        jnp.zeros((N_MICRO + 1, ROWS, D), BF),
    ]
    slopes = jnp.zeros((N_MICRO + 1, ROWS, D), BF)
    up_core, up_chip = [blank], [blank, blank]
    down_core, down_chip = [blank], [blank, blank]
    kept = None
    for tick in range(LAST + TICKS):
        if tick < TICKS:
            msg, *stash = forward_tick(
                tick, tab, ends, up_core[tick], up_chip[tick], held, full, gain_pair, stash
            )
            if tick < TICKS - 1:
                up_core.append(send(msg, UP_CORE))
            if tick < TICKS - 2:
                up_chip.append(send(msg, UP_CHIP))
            if tick == TICKS - 1:
                kept = send(stash[2][:N_MICRO].reshape(-1, D), TURN)
        if tick >= LAST:
            step = tick - LAST
            msg, stash[0], stash[1], slopes = backward_tick(
                step, tab, ends, down_core[step], down_chip[step], full, gain_pair, stash[:2], slopes
            )
            if step < TICKS - 1:
                down_core.append(send(msg, DOWN_CORE))
            if step < TICKS - 2:
                down_chip.append(send(msg, DOWN_CHIP))

    shard = scatter_grad(place, (stash[3], slopes))
    return (kept[None], shard[None])


def solution(mesh):
    in_specs = (
        P("dp", None),
        P("dp", None),
        P("section", None, "dp", None, None),
        P("dp"),
        P("dp"),
        P("section", "dp", None),
        P("section", None),
    )
    out_specs = (P("section", "dp", None), P("section", "dp", None))
    return jax.shard_map(body, mesh=mesh, in_specs=in_specs, out_specs=out_specs, check_vma=False)
```

time: 553 us -> 538 us (0.973)
  local copies, waits for them, and re-layouts: 15.3 us -> 87.7 us
  waiting for transfers between devices: 228 us -> 175 us
  Pallas kernels: 139 us -> 107 us
  starting transfers between devices: 129 us -> 146 us
  between operations: 15.2 us -> 2.55 us
  matrix products: 6.83 us -> 0 us
    ppermute x60 -> x91, waiting for transfers between devices: 59.3 us -> 175 us  [send(): return lax.ppermute(array, BOTH, pairs)]
    reduce_scatter x1 -> x0, waiting for transfers between devices: 84.8 us -> none  [body(): lax.psum_scatter(product, 'dp', scatter_dimension=0, tiled=True, axis_ind...]
    all_gather x2 -> x0, waiting for transfers between devices: 83.4 us -> none  [the longest x1 53.6 us: body(): lax.all_gather(rows, 'dp', axis=0, tiled=True, axis_index_groups=Z_GROUPS)]
    unnamed x15 -> x131, local copies, waits for them, and re-layouts: 3.06 us -> 78.6 us
    pallas_call x14, Pallas kernels: 73.9 us -> 24.7 us  [backward_tick(): pl.pallas_call(functools.partial(backward_kernel, tick), grid_spec=pltpu....]
    ppermute x60 -> x91, starting transfers between devices: 129 us -> 146 us  [send(): return lax.ppermute(array, BOTH, pairs)]
    pallas_call x0 -> x19, Pallas kernels: none -> 16.1 us  [the longest x16 7.41 us: product(): pl.pallas_call(functools.partial(product_kernel, len(arrived)), grid=(1,)...]
    dot_general x1 -> x0, matrix products: 6.83 us -> none  [body(): lax.dot_general(normed, slope, (((0,), (0,)), ((), ())), preferred_elemen...]
  transfers between devices with their start and end apart: 63 -> 91, of which waited for: 23 -> 37; matrix products, arithmetic and copies ran while one was open for 3% -> 3% of each run, Pallas kernels for 24% -> 19%
where the time goes in v2:
time: 538 us; the launch traced here: 528 us
  waiting for transfers between devices  175 us (33%)
  starting transfers between devices  146 us (27%)
  Pallas kernels  107 us (20%)
  local copies, waits for them, and re-layouts  87.7 us (16%)
  other arithmetic  8.78 us (2%)
    ppermute x91, waiting for transfers between devices, send(): return lax.ppermute(array, BOTH, pairs)  175 us
    ppermute x91, starting transfers between devices, send(): return lax.ppermute(array, BOTH, pairs)  146 us
    unnamed x131, local copies, waits for them, and re-layouts  78.6 us
    pallas_call x14, Pallas kernels, forward_tick(): pl.pallas_call(functools.partial(forward_kernel, tick), grid_spec=pltpu.P...  66.1 us
    pallas_call x14, Pallas kernels, backward_tick(): pl.pallas_call(functools.partial(backward_kernel, tick), grid_spec=pltpu....  24.7 us
  transfers between devices with their start and end apart: 91, of which 37 were waited for; matrix products, arithmetic and copies ran while one was open for 3% of the time, Pallas kernels for 19%

profile of v2, /device:TPU:1, one launch (start us, length us, event | category | flops | bytes accessed | tf_op | source)
XLA Modules:
  0.0 527.5 jit_solution(10548987074503847646)
XLA Ops:
  0.6 4.5 collective-permute-start.3
  8.8 3.3 broadcast_select_fusion
  25.7 4.0 collective-permute-start.8
  31.6 10.8 %collective-permute-done.13.refs_14_ = bf16[256,1024]{1,0:T(8,128)(2,1)S(1)} collective-permute-done((bf16[256,1024]{1,0:T(8,128)(2,1)}, bf16[256,1024]{1,0:T(8,128)(2,1)S(1)}, u32[]{:S(2)}, u32[]{:S(2)}) %collective-permute-start.13) | collective-permute-done | bytes 524320 | tf_op jit(solution)/shard_map/ppermute | solution.py:58
  46.4 6.3 %collective-permute-done.7.refs_2_ = bf16[256,1024]{1,0:T(8,128)(2,1)} collective-permute-done((bf16[256,1024]{1,0:T(8,128)(2,1)S(1)}, bf16[256,1024]{1,0:T(8,128)(2,1)}, u32[]{:S(2)}, u32[]{:S(2)}) %collective-permute-start.7) | collective-permute-done | bytes 524320 | tf_op jit(solution)/shard_map/ppermute | solution.py:58
  52.6 3.5 collective-permute-start.10
  56.2 8.5 %collective-permute-done.14.refs_12_ = bf16[256,1024]{1,0:T(8,128)(2,1)S(1)} collective-permute-done((bf16[256,1024]{1,0:T(8,128)(2,1)S(1)}, bf16[256,1024]{1,0:T(8,128)(2,1)S(1)}, u32[]{:S(2)}, u32[]{:S(2)}) %collective-permute-start.14) | collective-permute-done | bytes 524320 | tf_op jit(solution)/shard_map/ppermute | solution.py:58
  67.7 10.6 %collective-permute-done.9.refs_4_ = bf16[256,1024]{1,0:T(8,128)(2,1)} collective-permute-done((bf16[256,1024]{1,0:T(8,128)(2,1)}, bf16[256,1024]{1,0:T(8,128)(2,1)}, u32[]{:S(2)}, u32[]{:S(2)}) %collective-permute-start.9) | collective-permute-done | bytes 524320 | tf_op jit(solution)/shard_map/ppermute | solution.py:58
  78.3 3.4 collective-permute-start.12
  82.1 9.3 %collective-permute-done.15.refs_10_ = bf16[256,1024]{1,0:T(8,128)(2,1)} collective-permute-done((bf16[256,1024]{1,0:T(8,128)(2,1)}, bf16[256,1024]{1,0:T(8,128)(2,1)}, u32[]{:S(2)}, u32[]{:S(2)}) %collective-permute-start.15) | collective-permute-done | bytes 524320 | tf_op jit(solution)/shard_map/ppermute | solution.py:58
  93.5 9.5 %collective-permute-done.11.refs_6_ = bf16[256,1024]{1,0:T(8,128)(2,1)} collective-permute-done((bf16[256,1024]{1,0:T(8,128)(2,1)}, bf16[256,1024]{1,0:T(8,128)(2,1)}, u32[]{:S(2)}, u32[]{:S(2)}) %collective-permute-start.11) | collective-permute-done | bytes 524320 | tf_op jit(solution)/shard_map/ppermute | solution.py:58
  108.2 10.1 %collective-permute-done.16.refs_8_ = bf16[256,1024]{1,0:T(8,128)(2,1)S(1)} collective-permute-done((bf16[256,1024]{1,0:T(8,128)(2,1)}, bf16[256,1024]{1,0:T(8,128)(2,1)S(1)}, u32[]{:S(2)}, u32[]{:S(2)}) %collective-permute-start.16) | collective-permute-done | bytes 524320 | tf_op jit(solution)/shard_map/ppermute | solution.py:58
  121.2 3.4 copy-done
  127.8 4.0 forward_0.1
  133.1 5.3 collective-permute-start.24
  138.7 6.0 %forward_1.1 = (bf16[128,2048]{1,0:T(8,128)(2,1)S(1)}, bf16[5,128,2048]{2,1,0:T(8,128)(2,1)S(1)}, f32[5,128,2048]{2,1,0:T(8,128)S(1)}, bf16[5,128,2048]{2,1,0:T(8,128)(2,1)S(1)}, bf16[5,128,2048]{2,1,0:T(8,128)(2,1)S(1)}) custom-call(s32[19]{0:T(128)S(1)} %concatenate.6.tab, ...), custom_call_target="tpu_custom_call", output_to_operand_aliasing={{1}: (7, {}), {2}: (8, {}), {3}: (9, {}), {4}: (10, {})} | custom-call | flops 1073741824 | bytes 8388608 | tf_op jit(solution)/shard_map/forward_1/pallas_call | solution.py:259
  148.4 6.2 %forward_2.1 = (bf16[128,2048]{1,0:T(8,128)(2,1)S(1)}, bf16[5,128,2048]{2,1,0:T(8,128)(2,1)S(1)}, f32[5,128,2048]{2,1,0:T(8,128)S(1)}, bf16[5,128,2048]{2,1,0:T(8,128)(2,1)S(1)}, bf16[5,128,2048]{2,1,0:T(8,128)(2,1)S(1)}) custom-call(s32[19]{0:T(128)S(1)} %concatenate.6.tab, ...), custom_call_target="tpu_custom_call", output_to_operand_aliasing={{1}: (7, {}), {2}: (8, {}), {3}: (9, {}), {4}: (10, {})} | custom-call | flops 1073741824 | bytes 8388608 | tf_op jit(solution)/shard_map/forward_2/pallas_call | solution.py:259
  158.5 6.0 %forward_3.1 = (bf16[128,2048]{1,0:T(8,128)(2,1)S(1)}, bf16[5,128,2048]{2,1,0:T(8,128)(2,1)S(1)}, f32[5,128,2048]{2,1,0:T(8,128)S(1)}, bf16[5,128,2048]{2,1,0:T(8,128)(2,1)S(1)}, bf16[5,128,2048]{2,1,0:T(8,128)(2,1)S(1)}) custom-call(s32[19]{0:T(128)S(1)} %concatenate.6.tab, ...), custom_call_target="tpu_custom_call", output_to_operand_aliasing={{1}: (7, {}), {2}: (8, {}), {3}: (9, {}), {4}: (10, {})} | custom-call | flops 1073741824 | bytes 8388608 | tf_op jit(solution)/shard_map/forward_3/pallas_call | solution.py:259
  168.3 6.0 %forward_4.1 = (bf16[128,2048]{1,0:T(8,128)(2,1)S(1)}, bf16[5,128,2048]{2,1,0:T(8,128)(2,1)S(1)}, f32[5,128,2048]{2,1,0:T(8,128)S(1)}, bf16[5,128,2048]{2,1,0:T(8,128)(2,1)S(1)}, bf16[5,128,2048]{2,1,0:T(8,128)(2,1)S(1)}) custom-call(s32[19]{0:T(128)S(1)} %concatenate.6.tab, ...), custom_call_target="tpu_custom_call", output_to_operand_aliasing={{1}: (7, {}), {2}: (8, {}), {3}: (9, {}), {4}: (10, {})} | custom-call | flops 1073741824 | bytes 8388608 | tf_op jit(solution)/shard_map/forward_4/pallas_call | solution.py:259
  178.1 4.0 forward_5.1
  185.8 4.0 forward_6.1
  191.1 4.5 collective-permute-start.36
  195.6 4.3 forward_7.1
  201.3 4.5 collective-permute-start.38
  205.8 4.0 forward_8.1
  213.6 4.0 forward_9.1
  234.8 4.2 forward_10.1
  251.6 3.2 collective-permute-start.45
  261.2 4.2 forward_11.1
  279.6 3.3 collective-permute-start.47
  288.8 4.2 forward_12.1
  315.7 5.2 forward_13.1
  336.3 4.8 collective-permute-done.56.chip_ref
  362.7 14.1 %collective-permute-done.64.chip_ref = bf16[128,2048]{1,0:T(8,128)(2,1)S(1)} collective-permute-done((bf16[128,2048]{1,0:T(8,128)(2,1)S(1)}, bf16[128,2048]{1,0:T(8,128)(2,1)S(1)}, u32[]{:S(2)}, u32[]{:S(2)}) %collective-permute-start.64) | collective-permute-done | bytes 524320 | tf_op jit(solution)/shard_map/ppermute | solution.py:58
  376.9 4.5 backward_9.1
  385.0 4.4 backward_10.1
  392.0 5.3 %collective-permute-done.68.chip_ref = bf16[128,2048]{1,0:T(8,128)(2,1)S(1)} collective-permute-done((bf16[128,2048]{1,0:T(8,128)(2,1)S(1)}, bf16[128,2048]{1,0:T(8,128)(2,1)S(1)}, u32[]{:S(2)}, u32[]{:S(2)}) %collective-permute-start.68) | collective-permute-done | bytes 524320 | tf_op jit(solution)/shard_map/ppermute | solution.py:58
  397.3 4.4 backward_11.1
  407.1 4.4 backward_12.1
  429.7 3.7 collective-permute-done.83.refs_0_
  437.6 10.4 %collective-permute-done.80.refs_0_ = bf16[256,1024]{1,0:T(8,128)(2,1)S(1)} collective-permute-done((bf16[256,1024]{1,0:T(8,128)(2,1)S(1)}, bf16[256,1024]{1,0:T(8,128)(2,1)S(1)}, u32[]{:S(2)}, u32[]{:S(2)}) %collective-permute-start.80) | collective-permute-done | bytes 524320 | tf_op jit(solution)/shard_map/ppermute | solution.py:58
  451.9 4.0 collective-permute-done.84.refs_0_
  460.0 10.4 %collective-permute-done.81.refs_0_ = bf16[256,1024]{1,0:T(8,128)(2,1)S(1)} collective-permute-done((bf16[256,1024]{1,0:T(8,128)(2,1)S(1)}, bf16[256,1024]{1,0:T(8,128)(2,1)S(1)}, u32[]{:S(2)}, u32[]{:S(2)}) %collective-permute-start.81) | collective-permute-done | bytes 524320 | tf_op jit(solution)/shard_map/ppermute | solution.py:58
  471.4 7.0 %collective-permute-done.85.refs_0_ = bf16[256,1024]{1,0:T(8,128)(2,1)S(1)} collective-permute-done((bf16[256,1024]{1,0:T(8,128)(2,1)S(1)}, bf16[256,1024]{1,0:T(8,128)(2,1)S(1)}, u32[]{:S(2)}, u32[]{:S(2)}) %collective-permute-start.85) | collective-permute-done | bytes 524320 | tf_op jit(solution)/shard_map/ppermute | solution.py:58
  484.0 8.9 %collective-permute-done.82.refs_0_ = bf16[256,1024]{1,0:T(8,128)(2,1)S(1)} collective-permute-done((bf16[256,1024]{1,0:T(8,128)(2,1)S(1)}, bf16[256,1024]{1,0:T(8,128)(2,1)S(1)}, u32[]{:S(2)}, u32[]{:S(2)}) %collective-permute-start.82) | collective-permute-done | bytes 524320 | tf_op jit(solution)/shard_map/ppermute | solution.py:58
  494.2 9.2 %collective-permute-done.79.refs_1_ = bf16[256,1024]{1,0:T(8,128)(2,1)S(1)} collective-permute-done((bf16[256,1024]{1,0:T(8,128)(2,1)S(1)}, bf16[256,1024]{1,0:T(8,128)(2,1)S(1)}, u32[]{:S(2)}, u32[]{:S(2)}) %collective-permute-start.79) | collective-permute-done | bytes 524320 | tf_op jit(solution)/shard_map/ppermute | solution.py:58
  514.5 4.2 collective-permute-done.87
  519.6 5.3 %collective-permute-done.90 = bf16[64,2048]{1,0:T(8,128)(2,1)S(1)} collective-permute-done((bf16[64,2048]{1,0:T(8,128)(2,1)}, bf16[64,2048]{1,0:T(8,128)(2,1)S(1)}, u32[]{:S(2)}, u32[]{:S(2)}) %collective-permute-start.90) | collective-permute-done | bytes 262176 | tf_op jit(solution)/shard_map/ppermute | solution.py:58
  (348 shorter events, 246.1 us)
Async XLA Ops:
  0.6 18.5 %collective-permute-start.3 = (bf16[64,2048]{1,0:T(8,128)(2,1)}, bf16[64,2048]{1,0:T(8,128)(2,1)S(1)}, u32[]{:S(2)}, u32[]{:S(2)}) collective-permute-start(bf16[64,2048]{1,0:T(8,128)(2,1)} %bitcast.73), channel_id=1, source_target_pairs={{0,0},{1,32},{2,2},{3,34},{4,4},{5,36},{6,6},{7,38},{8,8},{9,40},{... | collective-permute-start | bytes 786440 | tf_op jit(solution)/shard_map/ppermute | solution.py:58
  5.5 15.0 %collective-permute-start.5 = (bf16[64,2048]{1,0:T(8,128)(2,1)}, bf16[64,2048]{1,0:T(8,128)(2,1)}, u32[]{:S(2)}, u32[]{:S(2)}) collective-permute-start(bf16[64,2048]{1,0:T(8,128)(2,1)} %bitcast.75), channel_id=1, source_target_pairs={{0,16},{1,48},{2,18},{3,50},{4,20},{5,52},{6,22},{7,54},{8,24},{9,... | collective-permute-start | bytes 786440 | tf_op jit(solution)/shard_map/ppermute | solution.py:58
  12.1 91.3 %collective-permute-start.1 = (bf16[512,2048]{1,0:T(8,128)(2,1)}, bf16[512,2048]{1,0:T(8,128)(2,1)}, u32[]{:S(2)}, u32[]{:S(2)}) collective-permute-start(bf16[512,2048]{1,0:T(8,128)(2,1)} %broadcast_select_fusion), channel_id=1, source_target_pairs={{0,1},{1,0},{2,3},{3,2},{4,5},{5,4},{6,7},{7,6},{8,9},{9,8},{10,11... | collective-permute-start | bytes 6291464 | tf_op jit(solution)/shard_map/ppermute | solution.py:58
  24.2 18.3 %collective-permute-start.13 = (bf16[256,1024]{1,0:T(8,128)(2,1)}, bf16[256,1024]{1,0:T(8,128)(2,1)S(1)}, u32[]{:S(2)}, u32[]{:S(2)}) collective-permute-start(bf16[256,1024]{1,0:T(8,128)(2,1)} %get-tuple-element.130.refs_0_), channel_id=1, source_target_pairs={{0,2},{1,3},{2,4},{3,5},{4,6},{5,7},{6,8},{7,9},{8,10},{9,11},{10,... | collective-permute-start | bytes 1572872 | tf_op jit(solution)/shard_map/ppermute | solution.py:58
  25.7 18.5 %collective-permute-start.8 = (bf16[256,1024]{1,0:T(8,128)(2,1)}, bf16[256,1024]{1,0:T(8,128)(2,1)}, u32[]{:S(2)}, u32[]{:S(2)}) collective-permute-start(bf16[256,1024]{1,0:T(8,128)(2,1)} %get-tuple-element.131.refs_1_), channel_id=1, source_target_pairs={{0,14},{1,15},{2,0},{3,1},{4,2},{5,3},{6,4},{7,5},{8,6},{9,7},{10,... | collective-permute-start | bytes 1572872 | tf_op jit(solution)/shard_map/ppermute | solution.py:58
  30.1 22.5 %collective-permute-start.7 = (bf16[256,1024]{1,0:T(8,128)(2,1)S(1)}, bf16[256,1024]{1,0:T(8,128)(2,1)}, u32[]{:S(2)}, u32[]{:S(2)}) collective-permute-start(bf16[256,1024]{1,0:T(8,128)(2,1)S(1)} %copy-done.45), channel_id=1, source_target_pairs={{0,14},{1,15},{2,0},{3,1},{4,2},{5,3},{6,4},{7,5},{8,6},{9,7},{10,... | collective-permute-start | bytes 1572872 | tf_op jit(solution)/shard_map/ppermute | solution.py:58
  31.6 24.6 %collective-permute-start.18 = (bf16[256,1024]{1,0:T(8,128)(2,1)S(1)}, bf16[256,1024]{1,0:T(8,128)(2,1)}, u32[]{:S(2)}, u32[]{:S(2)}) collective-permute-start(bf16[256,1024]{1,0:T(8,128)(2,1)S(1)} %copy-done.46), channel_id=1, source_target_pairs={{0,2},{1,3},{2,4},{3,5},{4,6},{5,7},{6,8},{7,9},{8,10},{9,11},{10,... | collective-permute-start | bytes 1572872 | tf_op jit(solution)/shard_map/ppermute | solution.py:58
  42.5 22.3 %collective-permute-start.14 = (bf16[256,1024]{1,0:T(8,128)(2,1)S(1)}, bf16[256,1024]{1,0:T(8,128)(2,1)S(1)}, u32[]{:S(2)}, u32[]{:S(2)}) collective-permute-start(bf16[256,1024]{1,0:T(8,128)(2,1)S(1)} %collective-permute-done.13.refs_14_), channel_id=1, source_target_pairs={{0,2},{1,3},{2,4},{3,5},{4,6},{5,7},{6,8},{7,9},{8,10},{9,11},{10,... | collective-permute-start | bytes 1572872 | tf_op jit(solution)/shard_map/ppermute | solution.py:58
  44.1 80.4 %collective-permute-start.2 = (bf16[512,2048]{1,0:T(8,128)(2,1)}, bf16[512,2048]{1,0:T(8,128)(2,1)S(1)}, u32[]{:S(2)}, u32[]{:S(2)}) collective-permute-start(bf16[512,2048]{1,0:T(8,128)(2,1)} %pad_maximum_fusion), channel_id=1, source_target_pairs={{0,0},{1,32},{2,2},{3,34},{4,4},{5,36},{6,6},{7,38},{8,8},{9,40},{... | collective-permute-start | bytes 6291464 | tf_op jit(solution)/shard_map/ppermute | solution.py:58
  56.1 22.2 %collective-permute-start.9 = (bf16[256,1024]{1,0:T(8,128)(2,1)}, bf16[256,1024]{1,0:T(8,128)(2,1)}, u32[]{:S(2)}, u32[]{:S(2)}) collective-permute-start(bf16[256,1024]{1,0:T(8,128)(2,1)} %collective-permute-done.7.refs_2_), channel_id=1, source_target_pairs={{0,14},{1,15},{2,0},{3,1},{4,2},{5,3},{6,4},{7,5},{8,6},{9,7},{10,... | collective-permute-start | bytes 1572872 | tf_op jit(solution)/shard_map/ppermute | solution.py:58
  65.6 16.2 %collective-permute-start.19 = (bf16[256,1024]{1,0:T(8,128)(2,1)}, bf16[256,1024]{1,0:T(8,128)(2,1)}, u32[]{:S(2)}, u32[]{:S(2)}) collective-permute-start(bf16[256,1024]{1,0:T(8,128)(2,1)} %collective-permute-done.18.refs_15_), channel_id=1, source_target_pairs={{0,2},{1,3},{2,4},{3,5},{4,6},{5,7},{6,8},{7,9},{8,10},{9,11},{10,... | collective-permute-start | bytes 1572872 | tf_op jit(solution)/shard_map/ppermute | solution.py:58
  67.1 24.4 %collective-permute-start.15 = (bf16[256,1024]{1,0:T(8,128)(2,1)}, bf16[256,1024]{1,0:T(8,128)(2,1)}, u32[]{:S(2)}, u32[]{:S(2)}) collective-permute-start(bf16[256,1024]{1,0:T(8,128)(2,1)} %copy-done.49), channel_id=1, source_target_pairs={{0,2},{1,3},{2,4},{3,5},{4,6},{5,7},{6,8},{7,9},{8,10},{9,11},{10,... | collective-permute-start | bytes 1572872 | tf_op jit(solution)/shard_map/ppermute | solution.py:58
  78.3 15.0 %collective-permute-start.12 = (bf16[256,1024]{1,0:T(8,128)(2,1)}, bf16[256,1024]{1,0:T(8,128)(2,1)}, u32[]{:S(2)}, u32[]{:S(2)}) collective-permute-start(bf16[256,1024]{1,0:T(8,128)(2,1)} %collective-permute-done.10.refs_5_), channel_id=1, source_target_pairs={{0,14},{1,15},{2,0},{3,1},{4,2},{5,3},{6,4},{7,5},{8,6},{9,7},{10,... | collective-permute-start | bytes 1572872 | tf_op jit(solution)/shard_map/ppermute | solution.py:58
  81.7 21.3 %collective-permute-start.11 = (bf16[256,1024]{1,0:T(8,128)(2,1)}, bf16[256,1024]{1,0:T(8,128)(2,1)}, u32[]{:S(2)}, u32[]{:S(2)}) collective-permute-start(bf16[256,1024]{1,0:T(8,128)(2,1)} %collective-permute-done.9.refs_4_), channel_id=1, source_target_pairs={{0,14},{1,15},{2,0},{3,1},{4,2},{5,3},{6,4},{7,5},{8,6},{9,7},{10,... | collective-permute-start | bytes 1572872 | tf_op jit(solution)/shard_map/ppermute | solution.py:58
  91.4 33.1 %collective-permute-start.21 = (bf16[1,2048]{1,0:T(2,128)(2,1)S(1)}, bf16[1,2048]{1,0:T(2,128)(2,1)S(1)}, u32[]{:S(2)}, u32[]{:S(2)}) collective-permute-start(bf16[1,2048]{1,0:T(2,128)(2,1)S(1)} %copy-done.55), channel_id=1, source_target_pairs={{0,0},{1,32},{2,2},{3,34},{4,4},{5,36},{6,6},{7,38},{8,8},{9,40},{... | collective-permute-start | bytes 12296 | tf_op jit(solution)/shard_map/ppermute | solution.py:58
  93.4 14.9 %collective-permute-start.20 = (bf16[256,1024]{1,0:T(8,128)(2,1)}, bf16[256,1024]{1,0:T(8,128)(2,1)S(1)}, u32[]{:S(2)}, u32[]{:S(2)}) collective-permute-start(bf16[256,1024]{1,0:T(8,128)(2,1)} %collective-permute-done.19.refs_13_), channel_id=1, source_target_pairs={{0,2},{1,3},{2,4},{3,5},{4,6},{5,7},{6,8},{7,9},{8,10},{9,11},{10,... | collective-permute-start | bytes 1572872 | tf_op jit(solution)/shard_map/ppermute | solution.py:58
  103.0 15.3 %collective-permute-start.16 = (bf16[256,1024]{1,0:T(8,128)(2,1)}, bf16[256,1024]{1,0:T(8,128)(2,1)S(1)}, u32[]{:S(2)}, u32[]{:S(2)}) collective-permute-start(bf16[256,1024]{1,0:T(8,128)(2,1)} %collective-permute-done.15.refs_10_), channel_id=1, source_target_pairs={{0,2},{1,3},{2,4},{3,5},{4,6},{5,7},{6,8},{7,9},{8,10},{9,11},{10,... | collective-permute-start | bytes 1572872 | tf_op jit(solution)/shard_map/ppermute | solution.py:58
  103.4 15.0 %collective-permute-start.17 = (bf16[256,1024]{1,0:T(8,128)(2,1)}, bf16[256,1024]{1,0:T(8,128)(2,1)S(1)}, u32[]{:S(2)}, u32[]{:S(2)}) collective-permute-start(bf16[256,1024]{1,0:T(8,128)(2,1)} %collective-permute-done.12.refs_7_), channel_id=1, source_target_pairs={{0,14},{1,15},{2,0},{3,1},{4,2},{5,3},{6,4},{7,5},{8,6},{9,7},{10,... | collective-permute-start | bytes 1572872 | tf_op jit(solution)/shard_map/ppermute | solution.py:58
  133.1 14.8 %collective-permute-start.24 = (bf16[128,2048]{1,0:T(8,128)(2,1)S(1)}, bf16[128,2048]{1,0:T(8,128)(2,1)S(1)}, u32[]{:S(2)}, u32[]{:S(2)}) collective-permute-start(bf16[128,2048]{1,0:T(8,128)(2,1)S(1)} %get-tuple-element.132), channel_id=1, source_target_pairs={{1,64},{3,66},{5,68},{7,70},{9,72},{11,74},{13,76},{15,78},{17,80}... | collective-permute-start | bytes 1572872 | tf_op jit(solution)/shard_map/ppermute | solution.py:58
  191.1 14.7 %collective-permute-start.36 = (bf16[128,2048]{1,0:T(8,128)(2,1)S(1)}, bf16[128,2048]{1,0:T(8,128)(2,1)S(1)}, u32[]{:S(2)}, u32[]{:S(2)}) collective-permute-start(bf16[128,2048]{1,0:T(8,128)(2,1)S(1)} %get-tuple-element.162), channel_id=1, source_target_pairs={{1,64},{3,66},{5,68},{7,70},{9,72},{11,74},{13,76},{15,78},{17,80}... | collective-permute-start | bytes 1572872 | tf_op jit(solution)/shard_map/ppermute | solution.py:58
  211.1 15.8 %collective-permute-start.40 = (bf16[128,2048]{1,0:T(8,128)(2,1)S(1)}, bf16[128,2048]{1,0:T(8,128)(2,1)S(1)}, u32[]{:S(2)}, u32[]{:S(2)}) collective-permute-start(bf16[128,2048]{1,0:T(8,128)(2,1)S(1)} %get-tuple-element.172), channel_id=1, source_target_pairs={{1,64},{3,66},{5,68},{7,70},{9,72},{11,74},{13,76},{15,78},{17,80}... | collective-permute-start | bytes 1572872 | tf_op jit(solution)/shard_map/ppermute | solution.py:58
  224.1 32.5 %collective-permute-start.42 = (bf16[128,2048]{1,0:T(8,128)(2,1)S(1)}, bf16[128,2048]{1,0:T(8,128)(2,1)S(1)}, u32[]{:S(2)}, u32[]{:S(2)}) collective-permute-start(bf16[128,2048]{1,0:T(8,128)(2,1)S(1)} %get-tuple-element.177), channel_id=1, source_target_pairs={{1,64},{3,66},{5,68},{7,70},{9,72},{11,74},{13,76},{15,78},{17,80}... | collective-permute-start | bytes 1572872 | tf_op jit(solution)/shard_map/ppermute | solution.py:58
  251.6 20.1 %collective-permute-start.45 = (bf16[128,2048]{1,0:T(8,128)(2,1)S(1)}, bf16[128,2048]{1,0:T(8,128)(2,1)S(1)}, u32[]{:S(2)}, u32[]{:S(2)}) collective-permute-start(bf16[128,2048]{1,0:T(8,128)(2,1)S(1)} %get-tuple-element.190), channel_id=1, source_target_pairs={{1,0},{3,2},{5,4},{7,6},{9,8},{11,10},{13,12},{15,14},{17,16},{19,... | collective-permute-start | bytes 1572872 | tf_op jit(solution)/shard_map/ppermute | solution.py:58
  254.9 28.1 %collective-permute-start.44 = (bf16[128,2048]{1,0:T(8,128)(2,1)S(1)}, bf16[128,2048]{1,0:T(8,128)(2,1)S(1)}, u32[]{:S(2)}, u32[]{:S(2)}) collective-permute-start(bf16[128,2048]{1,0:T(8,128)(2,1)S(1)} %get-tuple-element.182), channel_id=1, source_target_pairs={{1,64},{3,66},{5,68},{7,70},{9,72},{11,74},{13,76},{15,78},{17,80}... | collective-permute-start | bytes 1572872 | tf_op jit(solution)/shard_map/ppermute | solution.py:58
  269.1 15.1 %collective-permute-start.43 = (bf16[128,2048]{1,0:T(8,128)(2,1)S(1)}, bf16[128,2048]{1,0:T(8,128)(2,1)S(1)}, u32[]{:S(2)}, u32[]{:S(2)}) collective-permute-start(bf16[128,2048]{1,0:T(8,128)(2,1)S(1)} %get-tuple-element.189), channel_id=1, source_target_pairs={{0,1},{2,3},{4,5},{6,7},{8,9},{10,11},{12,13},{14,15},{16,17},{18,... | collective-permute-start | bytes 1572872 | tf_op jit(solution)/shard_map/ppermute | solution.py:58
  270.4 29.2 %collective-permute-start.49 = (bf16[128,2048]{1,0:T(8,128)(2,1)S(1)}, bf16[128,2048]{1,0:T(8,128)(2,1)S(1)}, u32[]{:S(2)}, u32[]{:S(2)}) collective-permute-start(bf16[128,2048]{1,0:T(8,128)(2,1)S(1)} %get-tuple-element.190), channel_id=1, source_target_pairs={{64,1},{66,3},{68,5},{70,7},{72,9},{74,11},{76,13},{78,15},{80,17}... | collective-permute-start | bytes 1572872 | tf_op jit(solution)/shard_map/ppermute | solution.py:58
  277.1 22.5 %collective-permute-start.48 = (bf16[128,2048]{1,0:T(8,128)(2,1)S(1)}, bf16[128,2048]{1,0:T(8,128)(2,1)S(1)}, u32[]{:S(2)}, u32[]{:S(2)}) collective-permute-start(bf16[128,2048]{1,0:T(8,128)(2,1)S(1)} %get-tuple-element.199), channel_id=1, source_target_pairs={{1,0},{3,2},{5,4},{7,6},{9,8},{11,10},{13,12},{15,14},{17,16},{19,... | collective-permute-start | bytes 1572872 | tf_op jit(solution)/shard_map/ppermute | solution.py:58
  279.6 29.8 %collective-permute-start.47 = (bf16[128,2048]{1,0:T(8,128)(2,1)S(1)}, bf16[128,2048]{1,0:T(8,128)(2,1)S(1)}, u32[]{:S(2)}, u32[]{:S(2)}) collective-permute-start(bf16[128,2048]{1,0:T(8,128)(2,1)S(1)} %get-tuple-element.189), channel_id=1, source_target_pairs={{1,64},{3,66},{5,68},{7,70},{9,72},{11,74},{13,76},{15,78},{17,80}... | collective-permute-start | bytes 1572872 | tf_op jit(solution)/shard_map/ppermute | solution.py:58
  283.0 43.2 %collective-permute-start.52 = (bf16[128,2048]{1,0:T(8,128)(2,1)S(1)}, bf16[128,2048]{1,0:T(8,128)(2,1)S(1)}, u32[]{:S(2)}, u32[]{:S(2)}) collective-permute-start(bf16[128,2048]{1,0:T(8,128)(2,1)S(1)} %get-tuple-element.199), channel_id=1, source_target_pairs={{64,1},{66,3},{68,5},{70,7},{72,9},{74,11},{76,13},{78,15},{80,17}... | collective-permute-start | bytes 1572872 | tf_op jit(solution)/shard_map/ppermute | solution.py:58
  305.0 21.2 %collective-permute-start.51 = (bf16[128,2048]{1,0:T(8,128)(2,1)S(1)}, bf16[128,2048]{1,0:T(8,128)(2,1)S(1)}, u32[]{:S(2)}, u32[]{:S(2)}) collective-permute-start(bf16[128,2048]{1,0:T(8,128)(2,1)S(1)} %get-tuple-element.209), channel_id=1, source_target_pairs={{1,0},{3,2},{5,4},{7,6},{9,8},{11,10},{13,12},{15,14},{17,16},{19,... | collective-permute-start | bytes 1572872 | tf_op jit(solution)/shard_map/ppermute | solution.py:58
  308.1 23.8 %collective-permute-start.54 = (bf16[128,2048]{1,0:T(8,128)(2,1)S(1)}, bf16[128,2048]{1,0:T(8,128)(2,1)S(1)}, u32[]{:S(2)}, u32[]{:S(2)}) collective-permute-start(bf16[128,2048]{1,0:T(8,128)(2,1)S(1)} %get-tuple-element.209), channel_id=1, source_target_pairs={{64,1},{66,3},{68,5},{70,7},{72,9},{74,11},{76,13},{78,15},{80,17}... | collective-permute-start | bytes 1572872 | tf_op jit(solution)/shard_map/ppermute | solution.py:58
  355.4 21.4 %collective-permute-start.64 = (bf16[128,2048]{1,0:T(8,128)(2,1)S(1)}, bf16[128,2048]{1,0:T(8,128)(2,1)S(1)}, u32[]{:S(2)}, u32[]{:S(2)}) collective-permute-start(bf16[128,2048]{1,0:T(8,128)(2,1)S(1)} %get-tuple-element.229), channel_id=1, source_target_pairs={{64,1},{66,3},{68,5},{70,7},{72,9},{74,11},{76,13},{78,15},{80,17}... | collective-permute-start | bytes 1572872 | tf_op jit(solution)/shard_map/ppermute | solution.py:58
  360.1 16.7 %collective-permute-start.63 = (bf16[128,2048]{1,0:T(8,128)(2,1)S(1)}, bf16[128,2048]{1,0:T(8,128)(2,1)S(1)}, u32[]{:S(2)}, u32[]{:S(2)}) collective-permute-start(bf16[128,2048]{1,0:T(8,128)(2,1)S(1)} %get-tuple-element.233), channel_id=1, source_target_pairs={{1,0},{3,2},{5,4},{7,6},{9,8},{11,10},{13,12},{15,14},{17,16},{19,... | collective-permute-start | bytes 1572872 | tf_op jit(solution)/shard_map/ppermute | solution.py:58
  361.4 23.6 %collective-permute-start.66 = (bf16[128,2048]{1,0:T(8,128)(2,1)S(1)}, bf16[128,2048]{1,0:T(8,128)(2,1)S(1)}, u32[]{:S(2)}, u32[]{:S(2)}) collective-permute-start(bf16[128,2048]{1,0:T(8,128)(2,1)S(1)} %get-tuple-element.233), channel_id=1, source_target_pairs={{64,1},{66,3},{68,5},{70,7},{72,9},{74,11},{76,13},{78,15},{80,17}... | collective-permute-start | bytes 1572872 | tf_op jit(solution)/shard_map/ppermute | solution.py:58
  382.7 14.6 %collective-permute-start.68 = (bf16[128,2048]{1,0:T(8,128)(2,1)S(1)}, bf16[128,2048]{1,0:T(8,128)(2,1)S(1)}, u32[]{:S(2)}, u32[]{:S(2)}) collective-permute-start(bf16[128,2048]{1,0:T(8,128)(2,1)S(1)} %get-tuple-element.237), channel_id=1, source_target_pairs={{64,1},{66,3},{68,5},{70,7},{72,9},{74,11},{76,13},{78,15},{80,17}... | collective-permute-start | bytes 1572872 | tf_op jit(solution)/shard_map/ppermute | solution.py:58
  390.7 16.3 %collective-permute-start.70 = (bf16[128,2048]{1,0:T(8,128)(2,1)S(1)}, bf16[128,2048]{1,0:T(8,128)(2,1)S(1)}, u32[]{:S(2)}, u32[]{:S(2)}) collective-permute-start(bf16[128,2048]{1,0:T(8,128)(2,1)S(1)} %get-tuple-element.241), channel_id=1, source_target_pairs={{64,1},{66,3},{68,5},{70,7},{72,9},{74,11},{76,13},{78,15},{80,17}... | collective-permute-start | bytes 1572872 | tf_op jit(solution)/shard_map/ppermute | solution.py:58
  424.0 90.5 %collective-permute-start.50 = (bf16[512,2048]{1,0:T(8,128)(2,1)}, bf16[512,2048]{1,0:T(8,128)(2,1)S(1)}, u32[]{:S(2)}, u32[]{:S(2)}) collective-permute-start(bf16[512,2048]{1,0:T(8,128)(2,1)} %bitcast.13), channel_id=1, source_target_pairs={{0,0},{1,32},{2,2},{3,34},{4,4},{5,36},{6,6},{7,38},{8,8},{9,40},{... | collective-permute-start | bytes 6291464 | tf_op jit(solution)/shard_map/ppermute | solution.py:58
  426.4 21.5 %collective-permute-start.80 = (bf16[256,1024]{1,0:T(8,128)(2,1)S(1)}, bf16[256,1024]{1,0:T(8,128)(2,1)S(1)}, u32[]{:S(2)}, u32[]{:S(2)}) collective-permute-start(bf16[256,1024]{1,0:T(8,128)(2,1)S(1)} %product_3_1.1), channel_id=1, source_target_pairs={{0,2},{1,3},{2,4},{3,5},{4,6},{5,7},{6,8},{7,9},{8,10},{9,11},{10,... | collective-permute-start | bytes 1572872 | tf_op jit(solution)/shard_map/ppermute | solution.py:58
  427.1 21.4 %collective-permute-start.77 = (bf16[256,1024]{1,0:T(8,128)(2,1)S(1)}, bf16[256,1024]{1,0:T(8,128)(2,1)S(1)}, u32[]{:S(2)}, u32[]{:S(2)}) collective-permute-start(bf16[256,1024]{1,0:T(8,128)(2,1)S(1)} %product_5_0.1), channel_id=1, source_target_pairs={{0,14},{1,15},{2,0},{3,1},{4,2},{5,3},{6,4},{7,5},{8,6},{9,7},{10,... | collective-permute-start | bytes 1572872 | tf_op jit(solution)/shard_map/ppermute | solution.py:58
  433.9 22.0 %collective-permute-start.84 = (bf16[256,1024]{1,0:T(8,128)(2,1)S(1)}, bf16[256,1024]{1,0:T(8,128)(2,1)S(1)}, u32[]{:S(2)}, u32[]{:S(2)}) collective-permute-start(bf16[256,1024]{1,0:T(8,128)(2,1)S(1)} %product_5_1.1), channel_id=1, source_target_pairs={{0,14},{1,15},{2,0},{3,1},{4,2},{5,3},{6,4},{7,5},{8,6},{9,7},{10,... | collective-permute-start | bytes 1572872 | tf_op jit(solution)/shard_map/ppermute | solution.py:58
  437.5 22.0 %collective-permute-start.74 = (bf16[256,1024]{1,0:T(8,128)(2,1)S(1)}, bf16[256,1024]{1,0:T(8,128)(2,1)S(1)}, u32[]{:S(2)}, u32[]{:S(2)}) collective-permute-start(bf16[256,1024]{1,0:T(8,128)(2,1)S(1)} %product_3_0.1), channel_id=1, source_target_pairs={{0,2},{1,3},{2,4},{3,5},{4,6},{5,7},{6,8},{7,9},{8,10},{9,11},{10,... | collective-permute-start | bytes 1572872 | tf_op jit(solution)/shard_map/ppermute | solution.py:58
  448.4 22.0 %collective-permute-start.81 = (bf16[256,1024]{1,0:T(8,128)(2,1)S(1)}, bf16[256,1024]{1,0:T(8,128)(2,1)S(1)}, u32[]{:S(2)}, u32[]{:S(2)}) collective-permute-start(bf16[256,1024]{1,0:T(8,128)(2,1)S(1)} %product_2_1.1), channel_id=1, source_target_pairs={{0,2},{1,3},{2,4},{3,5},{4,6},{5,7},{6,8},{7,9},{8,10},{9,11},{10,... | collective-permute-start | bytes 1572872 | tf_op jit(solution)/shard_map/ppermute | solution.py:58
  449.0 22.0 %collective-permute-start.78 = (bf16[256,1024]{1,0:T(8,128)(2,1)S(1)}, bf16[256,1024]{1,0:T(8,128)(2,1)S(1)}, u32[]{:S(2)}, u32[]{:S(2)}) collective-permute-start(bf16[256,1024]{1,0:T(8,128)(2,1)S(1)} %product_6_0.1), channel_id=1, source_target_pairs={{0,14},{1,15},{2,0},{3,1},{4,2},{5,3},{6,4},{7,5},{8,6},{9,7},{10,... | collective-permute-start | bytes 1572872 | tf_op jit(solution)/shard_map/ppermute | solution.py:58
  456.4 22.0 %collective-permute-start.85 = (bf16[256,1024]{1,0:T(8,128)(2,1)S(1)}, bf16[256,1024]{1,0:T(8,128)(2,1)S(1)}, u32[]{:S(2)}, u32[]{:S(2)}) collective-permute-start(bf16[256,1024]{1,0:T(8,128)(2,1)S(1)} %product_6_1.1), channel_id=1, source_target_pairs={{0,14},{1,15},{2,0},{3,1},{4,2},{5,3},{6,4},{7,5},{8,6},{9,7},{10,... | collective-permute-start | bytes 1572872 | tf_op jit(solution)/shard_map/ppermute | solution.py:58
  459.9 22.1 %collective-permute-start.75 = (bf16[256,1024]{1,0:T(8,128)(2,1)S(1)}, bf16[256,1024]{1,0:T(8,128)(2,1)S(1)}, u32[]{:S(2)}, u32[]{:S(2)}) collective-permute-start(bf16[256,1024]{1,0:T(8,128)(2,1)S(1)} %product_2_0.1), channel_id=1, source_target_pairs={{0,2},{1,3},{2,4},{3,5},{4,6},{5,7},{6,8},{7,9},{8,10},{9,11},{10,... | collective-permute-start | bytes 1572872 | tf_op jit(solution)/shard_map/ppermute | solution.py:58
  470.9 22.0 %collective-permute-start.82 = (bf16[256,1024]{1,0:T(8,128)(2,1)S(1)}, bf16[256,1024]{1,0:T(8,128)(2,1)S(1)}, u32[]{:S(2)}, u32[]{:S(2)}) collective-permute-start(bf16[256,1024]{1,0:T(8,128)(2,1)S(1)} %product_1_1.1), channel_id=1, source_target_pairs={{0,2},{1,3},{2,4},{3,5},{4,6},{5,7},{6,8},{7,9},{8,10},{9,11},{10,... | collective-permute-start | bytes 1572872 | tf_op jit(solution)/shard_map/ppermute | solution.py:58
  481.9 21.4 %collective-permute-start.79 = (bf16[256,1024]{1,0:T(8,128)(2,1)S(1)}, bf16[256,1024]{1,0:T(8,128)(2,1)S(1)}, u32[]{:S(2)}, u32[]{:S(2)}) collective-permute-start(bf16[256,1024]{1,0:T(8,128)(2,1)S(1)} %product_7_0.1), channel_id=1, source_target_pairs={{0,14},{1,15},{2,0},{3,1},{4,2},{5,3},{6,4},{7,5},{8,6},{9,7},{10,... | collective-permute-start | bytes 1572872 | tf_op jit(solution)/shard_map/ppermute | solution.py:58
  482.5 21.6 %collective-permute-start.76 = (bf16[256,1024]{1,0:T(8,128)(2,1)S(1)}, bf16[256,1024]{1,0:T(8,128)(2,1)S(1)}, u32[]{:S(2)}, u32[]{:S(2)}) collective-permute-start(bf16[256,1024]{1,0:T(8,128)(2,1)S(1)} %product_1_0.1), channel_id=1, source_target_pairs={{0,2},{1,3},{2,4},{3,5},{4,6},{5,7},{6,8},{7,9},{8,10},{9,11},{10,... | collective-permute-start | bytes 1572872 | tf_op jit(solution)/shard_map/ppermute | solution.py:58
  (108 other events, 887.4 us)
